TPU v7x, 32 devices: a whole 2x2x4 slice. The times are simulated.
32 devices in a mesh: lineage: 2 (over x), cells: 4 (over y, core), cols: 4 (over z).
Axes of the slice: x: 2, y: 2, z: 4, core: 2. Of those that a mesh axis runs over, the one named last changes fastest.
Arguments:
- positions: bfloat16 [128, 64, 512], P(('lineage', 'cells')), parts along dimension 0, may hold values from -1.5 to 1.5
- scales: bfloat16 [128, 512], P(('lineage', 'cells')), parts along dimension 0, may hold values from 1 to 2
- start_vectors: bfloat16 [128, 64, 512], P(('lineage', 'cells')), parts along dimension 0, may hold values from -6 to 6
- send_list: int32 [8, 4, 2], P(('lineage', 'cells')), parts along dimension 0, may hold values from 0 to 16, as said below
- pair_rows: int32 [8, 4, 48], P(('lineage', 'cells'), 'cols'), parts along dimension 0, may hold values from 0 to 15, as said below
- pair_partner: int32 [8, 4, 48], P(('lineage', 'cells'), 'cols'), parts along dimension 0, may hold values from 0 to 23, as said below
Outputs:
- subspace: float32 [128, 64, 512], P(('lineage', 'cells'), 'cols'), parts along dimension 0
There are 2 independent parts, one for each index of `lineage`. A program takes and returns all parts, laid end to end along the dimension named above; each array names one. Nothing has to cross between parts.
Inputs may be any that keep to these rules, and one draw needn't show every extreme that they name: `send_list`: entries are local blocks of the sending group, distinct within one (sender, receiver) list and filling its first slots; 16 marks an empty slot; a group's slots for itself are empty; some group receives a full list from every other group and every group does from the group before it. `pair_rows`: every block of a cells group is paired with itself on some device of the group. `pair_partner`: A value of 16 or more always names a filled slot, and every filled slot a group receives is named by some pair of that group.
All inputs are finite; a program needn't handle non-finite values.
Results may differ from a plain program's by a relative error of at most 0.0047.
Values may be sent and summed in bfloat16 or wider, within the bound.
No kernel may reach another device: no remote copies, remote signals or barrier semaphores. Data moves between devices by JAX's collectives and lax.ppermute only.
A program may use at most 128 MiB of HBM per device.

v0:
```python
import jax
import jax.numpy as jnp
from jax import lax
from jax.sharding import PartitionSpec as P

ITERS = 2


def kernel_tiles(points, spreads, square_norms, row_ids, partner_ids):
    left_points = jnp.take(points, row_ids, axis=0)
    right_points = jnp.take(points, partner_ids, axis=0)
    cross_terms = jnp.einsum(
        "gpi,gpj->gij", left_points, right_points, preferred_element_type=jnp.float32
    )
    distance = (
        jnp.take(square_norms, row_ids, axis=0)[:, :, None]
        + jnp.take(square_norms, partner_ids, axis=0)[:, None, :]
        - 2.0 * cross_terms
    )
    left_spread = jnp.take(spreads, row_ids, axis=0).astype(jnp.float32)
    right_spread = jnp.take(spreads, partner_ids, axis=0).astype(jnp.float32)
    kernel_width = left_spread[:, :, None] * right_spread[:, None, :]
    return jnp.exp(-distance / kernel_width).astype(jnp.bfloat16)


def orthonormalize(mapped, gram_matrix, vector_count):
    factor = jnp.linalg.cholesky(gram_matrix)
    inverse = lax.linalg.triangular_solve(
        factor, jnp.eye(vector_count, dtype=jnp.float32), left_side=True, lower=True
    )
    return jnp.einsum("kj,bjc->bkc", inverse, mapped, precision=lax.Precision.HIGHEST)


def body(positions, scales, start_vectors, send_list, pair_rows, pair_partner):
    blocks = positions.shape[0]
    width_block = positions.shape[2]
    vector_count = start_vectors.shape[1]
    peers = lax.axis_size("cells")
    capacity = send_list.shape[2]
    outgoing = send_list.reshape(-1)
    slot_count = outgoing.shape[0]
    row_ids = pair_rows.reshape(-1)
    partner_ids = pair_partner.reshape(-1)
    bundle = 4
    rounds = row_ids.shape[0] // bundle
    row_groups = row_ids.reshape(rounds, bundle)
    partner_groups = partner_ids.reshape(rounds, bundle)
    mirrored = (partner_groups != row_groups).astype(jnp.float32)
    share_rows = vector_count // lax.axis_size("cols")
    offset = lax.axis_index("cols") * share_rows
    cells_total = blocks * width_block * peers

    def pack(values):
        picked = jnp.take(values, outgoing, axis=0, mode="fill", fill_value=0)
        return picked.reshape((peers, capacity) + values.shape[1:])

    sent_points, sent_spreads = (
        lax.all_to_all(pack(positions), "cells", split_axis=0, concat_axis=0, tiled=True),
        lax.all_to_all(pack(scales), "cells", split_axis=0, concat_axis=0, tiled=True),
    )
    points = jnp.concatenate(
        [positions, sent_points.reshape((slot_count,) + positions.shape[1:])], axis=0
    )
    spreads = jnp.concatenate([scales, sent_spreads.reshape(slot_count, width_block)], axis=0)
    square_norms = jnp.einsum("bpi,bpi->bi", points, points, preferred_element_type=jnp.float32)

    def make_tiles(group_index):
        return kernel_tiles(
            points, spreads, square_norms, row_groups[group_index], partner_groups[group_index]
        )

    stored = lax.map(make_tiles, jnp.arange(rounds))

    def fetch_tiles(group_index):
        return stored[group_index]

    def degree_group(group_index, running):
        kernel = fetch_tiles(group_index)
        row_sums = jnp.sum(kernel, axis=2, dtype=jnp.float32)
        column_sums = jnp.sum(kernel, axis=1, dtype=jnp.float32) * mirrored[group_index][:, None]
        running = running.at[row_groups[group_index]].add(row_sums)
        return running.at[partner_groups[group_index]].add(column_sums)

    degree_terms = lax.fori_loop(
        0, rounds, degree_group, jnp.zeros((blocks + slot_count, width_block), jnp.float32)
    )
    returned = lax.all_to_all(
        degree_terms[blocks:].reshape(peers, capacity, width_block),
        "cells",
        split_axis=0,
        concat_axis=0,
        tiled=True,
    )
    own_degree = (
        degree_terms[:blocks]
        .at[outgoing]
        .add(returned.reshape(slot_count, width_block), mode="drop")
    )
    degree = lax.psum(own_degree, "cols")
    inverse_root = lax.rsqrt(degree)
    subspace = start_vectors.astype(jnp.float32)
    scaled = (inverse_root[:, None, :] * subspace).astype(jnp.bfloat16)
    for sweep_index in range(ITERS):
        arrived = lax.all_to_all(pack(scaled), "cells", split_axis=0, concat_axis=0, tiled=True)
        vectors = jnp.concatenate(
            [scaled, arrived.reshape(slot_count, vector_count, width_block)], axis=0
        )

        def vector_group(group_index, running):
            kernel = fetch_tiles(group_index)
            far_vectors = jnp.take(vectors, partner_groups[group_index], axis=0)
            row_vectors = jnp.take(vectors, row_groups[group_index], axis=0)
            forward = jnp.einsum(
                "gkj,gij->gki", far_vectors, kernel, preferred_element_type=jnp.float32
            )
            backward = (
                jnp.einsum("gki,gij->gkj", row_vectors, kernel, preferred_element_type=jnp.float32)
                * mirrored[group_index][:, None, None]
            )
            running = running.at[row_groups[group_index]].add(forward)
            return running.at[partner_groups[group_index]].add(backward)

        partials = lax.fori_loop(
            0,
            rounds,
            vector_group,
            jnp.zeros((blocks + slot_count, vector_count, width_block), jnp.float32),
        )
        back_terms = lax.all_to_all(
            partials[blocks:].reshape(peers, capacity, vector_count, width_block),
            "cells",
            split_axis=0,
            concat_axis=0,
            tiled=True,
        )
        own_terms = (
            partials[:blocks]
            .at[outgoing]
            .add(back_terms.reshape(slot_count, vector_count, width_block), mode="drop")
        )
        summed = lax.psum(own_terms, "cols")
        mapped = inverse_root[:, None, :] * summed
        gram_local = (
            jnp.einsum("bkc,bjc->kj", mapped, mapped, precision=lax.Precision.HIGHEST) / cells_total
        )
        gram_matrix = lax.psum(gram_local, "cells")
        subspace = orthonormalize(mapped, gram_matrix, vector_count)
        scaled = (inverse_root[:, None, :] * subspace).astype(jnp.bfloat16)
    return lax.dynamic_slice_in_dim(subspace, offset, share_rows, 1)


def solution(mesh):
    in_specs = (
        P(("lineage", "cells"), None, None),
        P(("lineage", "cells"), None),
        P(("lineage", "cells"), None, None),
        P(("lineage", "cells"), None, None),
        P(("lineage", "cells"), "cols", None),
        P(("lineage", "cells"), "cols", None),
    )
    out_specs = P(("lineage", "cells"), "cols", None)
    return jax.shard_map(body, mesh=mesh, in_specs=in_specs, out_specs=out_specs, check_vma=False)
```

profile of v0, /device:TPU:0, one launch (start us, length us, event | category | flops | bytes accessed | tf_op | source)
XLA Modules:
  0.0 798.2 jit_solution(1565530719136018799)
XLA Ops:
  10.3 4.2 all-to-all-start.1
  18.3 3.5 all-to-all-start
  23.9 6.7 all-to-all-done
  31.2 110.8 %while.49 = (s32[]{:T(128)}, bf16[12,4,512,512]{3,2,1,0:T(8,128)(2,1)}, s32[12]{0:T(128)S(1)}, s32[12,4]{1,0:T(8,128)S(1)}, f32[24,512]{1,0:T(8,128)S(1)}, /*ind...) while((s32[]{:T(128)}, ...), condition=%wide.region_1.6_spmd, body=%wide.region_0.5_spmd.sunk | while | flops 141834288 | bytes 3818367 | solution.py:72
  37.5 3.0 bitcast_dynamic-update-slice_fusion.2
  46.7 2.9 bitcast_dynamic-update-slice_fusion.2
  56.0 3.0 bitcast_dynamic-update-slice_fusion.2
  65.2 2.9 bitcast_dynamic-update-slice_fusion.2
  74.4 2.9 bitcast_dynamic-update-slice_fusion.2
  83.6 2.9 bitcast_dynamic-update-slice_fusion.2
  92.8 2.9 bitcast_dynamic-update-slice_fusion.2
  102.0 3.0 bitcast_dynamic-update-slice_fusion.2
  111.3 3.0 bitcast_dynamic-update-slice_fusion.2
  120.6 2.9 bitcast_dynamic-update-slice_fusion.2
  129.8 3.0 bitcast_dynamic-update-slice_fusion.2
  139.0 2.9 bitcast_dynamic-update-slice_fusion.2
  142.0 44.3 %while.50 = (s32[]{:T(128)}, f32[24,512]{1,0:T(8,128)S(1)}, s32[12,4]{1,0:T(8,128)S(1)}, bf16[12,4,512,512]{3,2,1,0:T(8,128)(2,1)}, s32[12,4]{1,0:T(8,128)S(1)}, /*index=5*/f32[12,4]{1,0:T(8,128)S(1)}, s32[]{:T(128)}) while((s32[]{:T(128)}, f32[24,512]{1,0:T(8,128)S(1)}, s32[12,4]{1,0:T(8,128)S(1)}, bf16[12,4,512,512]{3,2,1,0:T(8,128)(2,1)}, ...), condition=%wide.region_7.12_spmd, body=%wide.region_2.11_spmd.sunk | while | flops 3147802 | bytes 2196169 | solution.py:84
  186.9 3.3 all-to-all-start.2
  190.2 3.8 all-to-all-done.2
  194.7 19.8 %psum.35 = f32[16,512]{1,0:T(8,128)S(1)} all-reduce(f32[16,512]{1,0:T(8,128)S(1)} %scatter_fusion.5), channel_id=1, replica_groups=mesh['lineage'=2,'cells'=4,'cols'=4] {'cols'}, use_global_device_ids=true, to_apply=%region_9.14 | all-reduce | flops 8192 | bytes 65536 | tf_op jit(solution)/shard_map/psum | solution.py:99
  216.3 3.5 all-to-all-start.3
  219.7 8.8 %all-to-all-done.3 = bf16[4,2,64,512]{3,2,1,0:T(8,128)(2,1)S(1)} async-done(((bf16[4,2,64,512]{3,2,1,0:T(8,128)(2,1)}), bf16[4,2,64,512]{3,2,1,0:T(8,128)(2,1)S(1)}, u32[]{:S(2)}, u32[]{:S(2)}) %all-to-all-start.3) | async-done | bytes 524320 | tf_op jit(solution)/shard_map/all_to_all | solution.py:104
  230.8 132.1 %while.51 = (s32[]{:T(128)}, f32[24,64,512]{2,1,0:T(8,128)}, s32[12,4]{1,0:T(8,128)S(1)}, s32[12,4]{1,0:T(8,128)S(1)}, bf16[24,64,512]{2,1,0:T(8,128)(2,1)S(1)},...) while((s32[]{:T(128)}, f32[24,64,512]{2,1,0:T(8,128)}, s32[12,4]{1,0:T(8,128)S(1)}, ...), condition=%wide.region_13.18_spmd, body=%wide.region_10.17_spmd.sunk | while | flops 269092928 | bytes 9971073 | solution.py:123
  233.8 2.7 scatter_fusion.1
  239.2 2.7 scatter_fusion.2
  244.9 2.7 scatter_fusion.1
  261.2 2.7 scatter_fusion.2
  266.9 2.7 scatter_fusion.1
  272.3 2.7 scatter_fusion.2
  305.3 2.7 scatter_fusion.2
  316.3 2.7 scatter_fusion.2
  327.3 2.7 scatter_fusion.2
  338.3 2.7 scatter_fusion.2
  360.3 2.7 scatter_fusion.2
  365.4 4.2 all-to-all-start.4
  371.4 12.8 %all-to-all-done.4 = f32[4,2,64,512]{3,2,1,0:T(8,128)} async-done(((f32[4,2,64,512]{3,2,1,0:T(8,128)}), f32[4,2,64,512]{3,2,1,0:T(8,128)}, u32[]{:S(2)}, u32[]{:S(2)}) %all-to-all-start.4) | async-done | bytes 1048608 | tf_op jit(solution)/shard_map/all_to_all | solution.py:129
  384.2 3.7 scatter_fusion.6
  387.9 84.0 %all-reduce.3.cloned.1.call-done = f32[16,64,512]{2,1,0:T(8,128)} async-done(((f32[16,64,512]{2,1,0:T(8,128)}), f32[16,64,512]{2,1,0:T(8,128)}) %all-reduce.3.cloned.1.call-update) | async-done | bytes 2097168 | tf_op jit(solution)/shard_map/psum | solution.py:141
  471.9 4.3 fusion.83
  476.3 11.4 %psum.37 = f32[64,64]{0,1:T(8,128)S(1)} all-reduce(f32[64,64]{0,1:T(8,128)S(1)} %fusion.83), channel_id=1, replica_groups=mesh['lineage'=2,'cells'=4,'cols'=4] {'cells'}, use_global_device_ids=true, to_apply=%region_16.21 | all-reduce | flops 4096 | bytes 32768 | tf_op jit(solution)/shard_map/psum | solution.py:146
  487.8 5.8 cholesky.44
  495.0 4.9 custom-call.6
  503.8 3.5 all-to-all-start.5
  507.3 8.8 %all-to-all-done.5 = bf16[4,2,64,512]{3,2,1,0:T(8,128)(2,1)S(1)} async-done(((bf16[4,2,64,512]{3,2,1,0:T(8,128)(2,1)}), bf16[4,2,64,512]{3,2,1,0:T(8,128)(2,1)S(1)}, u32[]{:S(2)}, u32[]{:S(2)}) %all-to-all-start.5) | async-done | bytes 524320 | tf_op jit(solution)/shard_map/all_to_all | solution.py:104
  518.4 132.1 %while.52 = (s32[]{:T(128)}, f32[24,64,512]{2,1,0:T(8,128)}, s32[12,4]{1,0:T(8,128)S(1)}, s32[12,4]{1,0:T(8,128)S(1)}, bf16[24,64,512]{2,1,0:T(8,128)(2,1)S(1)},...) while((s32[]{:T(128)}, f32[24,64,512]{2,1,0:T(8,128)}, s32[12,4]{1,0:T(8,128)S(1)}, ...), condition=%wide.region_22.29_spmd, body=%wide.region_19.28_spmd.sunk | while | flops 269092928 | bytes 9971073 | solution.py:123
  521.4 2.7 scatter_fusion.3
  526.8 2.7 scatter_fusion.4
  532.4 2.7 scatter_fusion.3
  548.8 2.7 scatter_fusion.4
  554.5 2.7 scatter_fusion.3
  559.8 2.7 scatter_fusion.4
  592.8 2.7 scatter_fusion.4
  603.8 2.7 scatter_fusion.4
  614.8 2.7 scatter_fusion.4
  625.9 2.7 scatter_fusion.4
  647.8 2.7 scatter_fusion.4
  652.9 4.3 all-to-all-start.6
  658.9 12.8 %all-to-all-done.6 = f32[4,2,64,512]{3,2,1,0:T(8,128)} async-done(((f32[4,2,64,512]{3,2,1,0:T(8,128)}), f32[4,2,64,512]{3,2,1,0:T(8,128)}, u32[]{:S(2)}, u32[]{:S(2)}) %all-to-all-start.6) | async-done | bytes 1048608 | tf_op jit(solution)/shard_map/all_to_all | solution.py:129
  671.7 3.6 scatter_fusion.7
  675.4 84.7 %all-reduce.5.cloned.1.call-done = f32[16,64,512]{2,1,0:T(8,128)} async-done(((f32[16,64,512]{2,1,0:T(8,128)}), f32[16,64,512]{2,1,0:T(8,128)}) %all-reduce.5.cloned.1.call-update) | async-done | bytes 2097168 | tf_op jit(solution)/shard_map/psum | solution.py:141
  760.1 4.3 fusion.80
  764.5 11.4 %psum.39 = f32[64,64]{0,1:T(8,128)S(1)} all-reduce(f32[64,64]{0,1:T(8,128)S(1)} %fusion.80), channel_id=1, replica_groups=mesh['lineage'=2,'cells'=4,'cols'=4] {'cells'}, use_global_device_ids=true, to_apply=%region_25.32 | all-reduce | flops 4096 | bytes 32768 | tf_op jit(solution)/shard_map/psum | solution.py:146
  776.0 5.8 cholesky.55
  783.1 4.9 custom-call.7
  (555 shorter events, 335.4 us)
Async XLA Ops:
  6.5 17.3 %copy-start.6 = (bf16[16,512]{1,0:T(8,128)(2,1)S(1)}, bf16[16,512]{1,0:T(8,128)(2,1)}, u32[]{:S(2)}) copy-start(bf16[16,512]{1,0:T(8,128)(2,1)} %param.26) | copy-start | bytes 49156
  6.5 24.1 %copy-start.4 = (bf16[16,64,512]{2,1,0:T(8,128)(2,1)S(1)}, bf16[16,64,512]{2,1,0:T(8,128)(2,1)}, u32[]{:S(2)}) copy-start(bf16[16,64,512]{2,1,0:T(8,128)(2,1)} %param.25) | copy-start | bytes 3145732
  6.5 15.8 %copy-start.7 = (s32[1,1,48]{2,1,0:T(1,128)S(1)}, s32[1,1,48]{2,1,0:T(1,128)}, u32[]{:S(2)}) copy-start(s32[1,1,48]{2,1,0:T(1,128)} %param.29) | copy-start | bytes 580
  6.5 16.6 %copy-start.8 = (s32[1,1,48]{2,1,0:T(1,128)S(1)}, s32[1,1,48]{2,1,0:T(1,128)}, u32[]{:S(2)}) copy-start(s32[1,1,48]{2,1,0:T(1,128)} %param.30) | copy-start | bytes 580
  10.3 8.1 %all-to-all-start.1 = ((bf16[4,2,512]{2,1,0:T(2,128)(2,1)}), bf16[4,2,512]{2,1,0:T(2,128)(2,1)S(1)}, u32[]{:S(2)}, u32[]{:S(2)}) async-start(bf16[4,2,512]{2,1,0:T(2,128)(2,1)} %broadcast_select_fusion.5), calls=%async_computation.1 | async-start | bytes 16384 | tf_op jit(solution)/shard_map/all_to_all | solution.py:59
  18.3 12.3 %all-to-all-start = ((bf16[4,2,64,512]{3,2,1,0:T(8,128)(2,1)}), bf16[4,2,64,512]{3,2,1,0:T(8,128)(2,1)S(1)}, u32[]{:S(2)}, u32[]{:S(2)}) async-start(bf16[4,2,64,512]{3,2,1,0:T(8,128)(2,1)} %bitcast.27), calls=%async_computation | async-start | bytes 1048576 | tf_op jit(solution)/shard_map/all_to_all | solution.py:58
  142.0 72.6 %copy-start.5 = (bf16[16,64,512]{2,1,0:T(8,128)(2,1)S(1)}, bf16[16,64,512]{2,1,0:T(8,128)(2,1)}, u32[]{:S(2)}) copy-start(bf16[16,64,512]{2,1,0:T(8,128)(2,1)} %param.27) | copy-start | bytes 3145732
  186.9 7.1 all-to-all-start.2
  216.3 12.3 %all-to-all-start.3 = ((bf16[4,2,64,512]{3,2,1,0:T(8,128)(2,1)}), bf16[4,2,64,512]{3,2,1,0:T(8,128)(2,1)S(1)}, u32[]{:S(2)}, u32[]{:S(2)}) async-start(bf16[4,2,64,512]{3,2,1,0:T(8,128)(2,1)} %bitcast.31), calls=%async_computation.3 | async-start | bytes 1048576 | tf_op jit(solution)/shard_map/all_to_all | solution.py:104
  363.0 6.8 copy-start.1
  365.4 18.8 %all-to-all-start.4 = ((f32[4,2,64,512]{3,2,1,0:T(8,128)}), f32[4,2,64,512]{3,2,1,0:T(8,128)}, u32[]{:S(2)}, u32[]{:S(2)}) async-start(f32[4,2,64,512]{3,2,1,0:T(8,128)} %bitcast.162), calls=%async_computation.4 | async-start | bytes 2097152 | tf_op jit(solution)/shard_map/all_to_all | solution.py:129
  369.7 102.2 %all-reduce.3.cloned.1.call-start = ((), (), s32[]{:S(2)}) async-start(), calls=%async_computation.7 | async-start | bytes 4194304 | tf_op jit(solution)/shard_map/psum | solution.py:141
  471.9 28.2 %copy-start.3 = (f32[16,64,512]{2,1,0:T(8,128)S(1)}, f32[16,64,512]{2,1,0:T(8,128)}, u32[]{:S(2)}) copy-start(f32[16,64,512]{2,1,0:T(8,128)} %all-reduce.3.cloned.1.call-done) | copy-start | bytes 6291460
  503.8 12.3 %all-to-all-start.5 = ((bf16[4,2,64,512]{3,2,1,0:T(8,128)(2,1)}), bf16[4,2,64,512]{3,2,1,0:T(8,128)(2,1)S(1)}, u32[]{:S(2)}, u32[]{:S(2)}) async-start(bf16[4,2,64,512]{3,2,1,0:T(8,128)(2,1)} %bitcast.41), calls=%async_computation.5 | async-start | bytes 1048576 | tf_op jit(solution)/shard_map/all_to_all | solution.py:104
  650.5 6.8 copy-start
  652.9 18.8 %all-to-all-start.6 = ((f32[4,2,64,512]{3,2,1,0:T(8,128)}), f32[4,2,64,512]{3,2,1,0:T(8,128)}, u32[]{:S(2)}, u32[]{:S(2)}) async-start(f32[4,2,64,512]{3,2,1,0:T(8,128)} %bitcast.163), calls=%async_computation.6 | async-start | bytes 2097152 | tf_op jit(solution)/shard_map/all_to_all | solution.py:129
  657.2 102.9 %all-reduce.5.cloned.1.call-start = ((), (), s32[]{:S(2)}) async-start(), calls=%async_computation.8 | async-start | bytes 4194304 | tf_op jit(solution)/shard_map/psum | solution.py:141
  760.1 28.2 %copy-start.2 = (f32[16,64,512]{2,1,0:T(8,128)S(1)}, f32[16,64,512]{2,1,0:T(8,128)}, u32[]{:S(2)}) copy-start(f32[16,64,512]{2,1,0:T(8,128)} %all-reduce.5.cloned.1.call-done) | copy-start | bytes 6291460
Sparse Core Ops, SparseCore 0:
  388.0 83.8 all-reduce.2
  675.5 84.5 all-reduce.4
where the time goes:
time: 802 us; the launch traced here: 798 us
  waiting for transfers between devices  224 us (28%)
  other arithmetic  215 us (27%)
  matrix products  156 us (19%)
  local copies, waits for them, and re-layouts  95.4 us (12%)
  blocking collectives  42.6 us (5%)
  starting transfers between devices  26.5 us (3%)
  loops' own time  25.6 us (3%)
  between operations  13.8 us (2%)
    psum x2, waiting for transfers between devices, body(): summed = lax.psum(own_terms, 'cols')  169 us
    scatter-add x24, other arithmetic, vector_group(): return running.at[partner_groups[group_index]].add(backward)  63.9 us
    scatter-add x24, other arithmetic, vector_group(): running = running.at[row_groups[group_index]].add(forward)  63.6 us
    dot_general x24, matrix products, vector_group(): jnp.einsum('gkj,gij->gki', far_vectors, kernel, preferred_element_type=jn...  56.5 us
    dot_general x24, matrix products, vector_group(): jnp.einsum('gki,gij->gkj', row_vectors, kernel, preferred_element_type=jn...  50.8 us
    dot_general x12, matrix products, kernel_tiles(): jnp.einsum('gpi,gpj->gij', left_points, right_points, preferred_element_t...  35.4 us
    reduce_sum x12, other arithmetic, degree_group(): jnp.sum(kernel, axis=1, dtype=jnp.float32) * mirrored[group_index][:, None]  27.3 us
    all_to_all x2, waiting for transfers between devices, body(): lax.all_to_all(partials[blocks:].reshape(peers, capacity, vector_count, w...  25.6 us
  transfers between devices with their start and end apart: 9, of which 9 were waited for; matrix products, arithmetic and copies ran while one was open for 1% of the time, Pallas kernels for 0%

commit v1 on v0

v1 whole, which is shorter than its diff:
```python
import math

import jax
import jax.numpy as jnp
from jax import lax
from jax.experimental import pallas as pl
from jax.experimental.pallas import tpu as pltpu
from jax.sharding import PartitionSpec as P

F32 = jnp.float32
BF16 = jnp.bfloat16
LOG2E = math.log2(math.e)
GROUP = 4
RING = 4
STORED = 160
DEPTH = 256
VMEM_BYTES = 56 * 2**20

VMEM_SPEC = pl.BlockSpec(memory_space=pltpu.VMEM)
SMEM_SPEC = pl.BlockSpec(memory_space=pltpu.SMEM)
ANY_SPEC = pl.BlockSpec(memory_space=pl.ANY)


def dot(a, b, ca, cb, precision=None):
    return lax.dot_general(
        a, b, (((ca,), (cb,)), ((), ())), preferred_element_type=F32, precision=precision
    )


def params():
    return pltpu.CompilerParams(vmem_limit_bytes=VMEM_BYTES)


def exchange(pieces, axis):
    n = lax.axis_size(axis)
    return [
        lax.ppermute(pieces[m], axis, [(i, i ^ m) for i in range(n)]) for m in range(1, n)
    ]


def spread(value, axis):
    n = lax.axis_size(axis)
    return [value] + [
        lax.ppermute(value, axis, [(i, (i + s) % n) for i in range(n)]) for s in range(1, n)
    ]


def butterfly(value, axis):
    n = lax.axis_size(axis)
    step = 1
    while step < n:
        value = value + lax.ppermute(value, axis, [(i, i ^ step) for i in range(n)])
        step *= 2
    return value


class Sizes:
    def __init__(self, positions, start, send_list, pair_rows):
        self.blocks, self.comps, self.width = positions.shape
        self.vectors = start.shape[1]
        self.peers = lax.axis_size("cells")
        self.cols = lax.axis_size("cols")
        self.cap = send_list.shape[2]
        self.slots = self.peers * self.cap
        self.own = self.blocks // self.cols
        self.pairs = pair_rows.shape[2] * self.cols
        self.long = 2 * self.pairs + GROUP
        self.short = self.pairs + GROUP
        self.r1, self.p1 = 0, self.long
        self.rs = 2 * self.long
        self.ps = self.rs + self.short
        self.r2 = self.ps + self.short
        self.p2 = self.r2 + self.short
        self.head = self.p2 + self.short
        self.mine = self.head + 8
        self.theirs = self.mine + self.slots
        self.table = self.theirs + self.slots


def build_table(sz, rows, partners, send_all, where):
    def kernel(rows_ref, partners_ref, send_ref, where_ref, tab):
        c = where_ref[0]
        z = where_ref[1]

        def lists(i, carry):
            m = i // sz.cap
            q = i % sz.cap
            tab[sz.mine + i] = send_ref[0, jnp.bitwise_xor(c, m) * sz.cap + q]
            tab[sz.theirs + i] = send_ref[m, c * sz.cap + q]
            return carry

        lax.fori_loop(0, sz.slots, lists, 0)

        def pair(i, carry):
            n1, ns, n2 = carry
            r = rows_ref[i]
            p = partners_ref[i]
            local = p < sz.blocks
            row_mine = (r // sz.own) == z
            slot = jnp.maximum(p - sz.blocks, 0)
            slot = jnp.bitwise_xor(slot // sz.cap, c) * sz.cap + slot % sz.cap
            slot_mine = (tab[sz.theirs + slot] // sz.own) == z
            base = z * sz.own
            tab[sz.r1 + n1] = r - base
            tab[sz.p1 + n1] = p
            n1 = n1 + jnp.where(jnp.logical_and(local, row_mine), 1, 0)
            tab[sz.r1 + n1] = p - base
            tab[sz.p1 + n1] = r
            both = jnp.logical_and(local, jnp.logical_and(p != r, (p // sz.own) == z))
            n1 = n1 + jnp.where(both, 1, 0)
            far = jnp.logical_not(local)
            tab[sz.r2 + n2] = r - base
            tab[sz.p2 + n2] = slot
            n2 = n2 + jnp.where(jnp.logical_and(far, row_mine), 1, 0)
            tab[sz.rs + ns] = slot
            tab[sz.ps + ns] = r
            ns = ns + jnp.where(jnp.logical_and(far, slot_mine), 1, 0)
            return n1, ns, n2

        zero = jnp.int32(0)
        n1, ns, n2 = lax.fori_loop(0, sz.pairs, pair, (zero, zero, zero))
        for i in range(GROUP):
            tab[sz.r1 + n1 + i] = sz.own
            tab[sz.p1 + n1 + i] = 0
            tab[sz.rs + ns + i] = sz.slots
            tab[sz.ps + ns + i] = 0
            tab[sz.r2 + n2 + i] = sz.own
            tab[sz.p2 + n2 + i] = 0
        tab[sz.head] = z
        tab[sz.head + 1] = (n1 + GROUP - 1) // GROUP
        tab[sz.head + 2] = (ns + GROUP - 1) // GROUP
        tab[sz.head + 3] = (n2 + GROUP - 1) // GROUP
        for i in range(4, 8):
            tab[sz.head + i] = 0

    return pl.pallas_call(
        kernel,
        out_shape=jax.ShapeDtypeStruct((sz.table,), jnp.int32),
        in_specs=[SMEM_SPEC] * 4,
        out_specs=SMEM_SPEC,
    )(rows, partners, send_all, where)


def split3(value):
    first = value.astype(BF16)
    rest = value - first.astype(F32)
    second = rest.astype(BF16)
    third = (rest - second.astype(F32)).astype(BF16)
    return first, second, third


def fill_factors(points, spread_row, left, right):
    comps = points.shape[0]
    x = points.astype(F32)
    inverse = 1.0 / spread_row
    norms = jnp.sum(x * x, axis=0, keepdims=True)
    y = x * (inverse * math.sqrt(2.0 * LOG2E))
    high = y.astype(BF16)
    low = (y - high.astype(F32)).astype(BF16)
    a1, a2, a3 = split3(norms * inverse * LOG2E)
    b1, b2, b3 = split3(inverse)
    left[0:comps] = high
    left[comps : 2 * comps] = low
    left[2 * comps : 3 * comps] = high
    right[0:comps] = high
    right[comps : 2 * comps] = high
    right[2 * comps : 3 * comps] = low
    rest = DEPTH - 3 * comps
    shape = (rest, points.shape[1])
    row = lax.broadcasted_iota(jnp.int32, shape, 0)
    lefts = (-a1, -a1, -a2, -a2, -a1, -a3, -b1, -b2, -b1, -b2, -b3, -b1)
    rights = (b1, b2, b1, b2, b3, b1, a1, a1, a2, a2, a1, a3)
    l_rest = jnp.zeros(shape, F32)
    r_rest = jnp.zeros(shape, F32)
    for k, (l_row, r_row) in enumerate(zip(lefts, rights)):
        l_rest = jnp.where(row == k, l_row.astype(F32), l_rest)
        r_rest = jnp.where(row == k, r_row.astype(F32), r_rest)
    left[3 * comps :] = l_rest.astype(BF16)
    right[3 * comps :] = r_rest.astype(BF16)


def segments(sz, tab, name):
    g1, gs, g2 = tab[sz.head + 1], tab[sz.head + 2], tab[sz.head + 3]
    if name == "1":
        return sz.r1, sz.p1, g1, 0
    if name == "S":
        return sz.rs, sz.ps, gs, g1
    return sz.r2, sz.p2, g2, g1 + gs


def row_block(sz, tab, name, row):
    if name == "S":
        return sz.blocks + jnp.minimum(row, sz.slots - 1)
    return tab[sz.head] * sz.own + jnp.minimum(row, sz.own - 1)


def partner_block(sz, name, partner):
    return sz.blocks + partner if name == "2" else partner


def build_tiles(sz, table, names, points, spreads, tiles, sums):
    first = tiles is None
    pieces = len(points)
    held = sz.blocks + (sz.slots if pieces > 1 else 0)
    sum_rows = sz.own + 1 + sz.slots + 1

    def kernel(*refs):
        tab = refs[0]
        point_refs = refs[1 : 1 + pieces]
        spread_refs = refs[1 + pieces : 1 + 2 * pieces]
        refs = refs[1 + 2 * pieces :]
        if not first:
            refs = refs[1:]
            old_sums, refs = refs[0], refs[1:]
        store, sum_ref, left, right, ring, sem = refs
        if first:
            sum_ref[...] = jnp.zeros(sum_ref.shape, F32)
        else:
            sum_ref[...] = old_sums[...]

        def local(b, carry):
            fill_factors(point_refs[0][b], spread_refs[0][b], left.at[b], right.at[b])
            return carry

        lax.fori_loop(0, sz.blocks, local, 0)
        for m in range(1, pieces):

            def far(q, carry, m=m):
                at = sz.blocks + m * sz.cap + q
                fill_factors(point_refs[m][q], spread_refs[m][q], left.at[at], right.at[at])
                return carry

            lax.fori_loop(0, sz.cap, far, 0)

        def write(slot, step):
            return pltpu.make_async_copy(
                ring.at[slot], store.at[pl.ds(step * GROUP, GROUP)], sem.at[slot]
            )

        done = jnp.int32(0)
        for name in names:
            rows, partners, steps, place = segments(sz, tab, name)
            base = 0 if name != "S" else sz.own + 1

            def step(t, carry, name=name, rows=rows, partners=partners, place=place, base=base, done=done):
                slot = lax.rem(done + t, 2)

                @pl.when(done + t >= 2)
                def _():
                    write(slot, 0).wait()

                for k in range(GROUP):
                    row = tab[rows + t * GROUP + k]
                    partner = tab[partners + t * GROUP + k]
                    r = row_block(sz, tab, name, row)
                    p = partner_block(sz, name, partner)
                    kernel_tile = jnp.exp2(dot(left[p], right[r], 0, 0))
                    ring[slot, k] = kernel_tile.astype(BF16)
                    sum_ref[base + row] += jnp.sum(
                        kernel_tile.reshape(sz.width // 8, 8, sz.width), axis=0
                    )
                write(slot, jnp.minimum(place + t, STORED // GROUP)).start()
                return carry

            lax.fori_loop(0, steps, step, 0)
            done = done + steps
        for slot in range(2):

            @pl.when(done >= slot + 1)
            def _(slot=slot):
                write(slot, 0).wait()

    tile_shape = jax.ShapeDtypeStruct((STORED + GROUP, sz.width, sz.width), BF16)
    sum_shape = jax.ShapeDtypeStruct((sum_rows, 8, sz.width), F32)
    args = [table] + points + spreads
    specs = [SMEM_SPEC] + [VMEM_SPEC] * (2 * pieces)
    aliases = {}
    if not first:
        aliases = {len(args): 0}
        args += [tiles, sums]
        specs += [ANY_SPEC, VMEM_SPEC]
    entries = 64 if first else 28
    return pl.pallas_call(
        kernel,
        out_shape=(tile_shape, sum_shape),
        in_specs=specs,
        out_specs=(ANY_SPEC, VMEM_SPEC),
        scratch_shapes=[
            pltpu.VMEM((held, DEPTH, sz.width), BF16),
            pltpu.VMEM((held, DEPTH, sz.width), BF16),
            pltpu.VMEM((2, GROUP, sz.width, sz.width), BF16),
            pltpu.SemaphoreType.DMA((2,)),
        ],
        input_output_aliases=aliases,
        compiler_params=params(),
        cost_estimate=pl.CostEstimate(
            flops=2 * entries * sz.width**2 * DEPTH,
            bytes_accessed=2 * entries * sz.width**2,
            transcendentals=entries * sz.width**2,
        ),
    )(*args)


def scale_start(sz, table, send_all, where, partial, start, start_far):
    def kernel(tab, send_ref, where_ref, *refs):
        parts = refs[: sz.peers]
        start_ref = refs[sz.peers]
        far_refs = refs[sz.peers + 1 : 2 * sz.peers]
        near_out, far_out, root_out, total = refs[2 * sz.peers :]
        c = where_ref[0]
        for m in range(sz.peers):
            total[m, 0 : sz.blocks] = parts[m][0 : sz.blocks]
        for m in range(sz.peers):
            for k in range(sz.peers):
                if k == m:
                    continue
                for q in range(sz.cap):
                    b = send_ref[m, jnp.bitwise_xor(c, k) * sz.cap + q]
                    at = sz.blocks + (k ^ m) * sz.cap + q
                    total[m, pl.ds(b, 1), :] += parts[k][at : at + 1, :]
        root = lax.rsqrt(total[0, 0 : sz.blocks])
        root_out[...] = root
        for b in range(sz.blocks):
            near_out[b] = (root[b : b + 1] * start_ref[b].astype(F32)).astype(BF16)
        far_out[0 : sz.cap] = jnp.zeros((sz.cap, sz.vectors, sz.width), BF16)
        for m in range(1, sz.peers):
            for q in range(sz.cap):
                b = jnp.minimum(tab[sz.theirs + m * sz.cap + q], sz.blocks - 1)
                far_root = lax.rsqrt(total[m, pl.ds(b, 1), :])
                far_out[m * sz.cap + q] = (far_root * far_refs[m - 1][q].astype(F32)).astype(BF16)

    return pl.pallas_call(
        kernel,
        out_shape=(
            jax.ShapeDtypeStruct((sz.blocks, sz.vectors, sz.width), BF16),
            jax.ShapeDtypeStruct((sz.slots, sz.vectors, sz.width), BF16),
            jax.ShapeDtypeStruct((sz.blocks, sz.width), F32),
        ),
        in_specs=[SMEM_SPEC] * 3 + [VMEM_SPEC] * (2 * sz.peers),
        out_specs=(VMEM_SPEC,) * 3,
        scratch_shapes=[pltpu.VMEM((sz.peers, sz.blocks + 8, sz.width), F32)],
        compiler_params=params(),
    )(table, send_all, where, *partial, start, *start_far)


def sweep_scratch(sz, held):
    return [
        pltpu.VMEM((held, sz.vectors, sz.width), BF16),
        pltpu.VMEM((RING, GROUP, sz.width, sz.width), BF16),
        pltpu.SemaphoreType.DMA((RING,)),
        pltpu.SemaphoreType.DMA((max(sz.cols, sz.peers),)),
        pltpu.VMEM((2, sz.comps, sz.width), BF16),
        pltpu.VMEM((2, 1, sz.width), F32),
        pltpu.VMEM((2, DEPTH, sz.width), BF16),
        pltpu.SemaphoreType.DMA((4,)),
    ]


class Stream:
    def __init__(self, sz, tab, name, store, geometry, scratch):
        self.sz, self.tab, self.name, self.store, self.geometry = sz, tab, name, store, geometry
        _, self.ring, self.sem, _, self.x, self.s, self.factors, self.xsem = scratch
        self.rows, self.partners, self.steps, self.place = segments(sz, tab, name)

    def read(self, t):
        slot = lax.rem(t, RING)
        return pltpu.make_async_copy(
            self.store.at[pl.ds((self.place + t) * GROUP, GROUP)], self.ring.at[slot], self.sem.at[slot]
        )

    def stored(self, t):
        return jnp.logical_and(t < self.steps, self.place + t < STORED // GROUP)

    def begin(self):
        for t in range(RING - 1):

            @pl.when(self.stored(t))
            def _(t=t):
                self.read(t).start()

    def rebuild(self, t):
        sz = self.sz
        slot = lax.rem(t, RING)

        def one(k, carry):
            row = self.tab[self.rows + t * GROUP + k]
            partner = self.tab[self.partners + t * GROUP + k]
            places = (
                partner_block(sz, self.name, partner),
                row_block(sz, self.tab, self.name, row),
            )
            for side, place in enumerate(places):
                copies = (
                    pltpu.make_async_copy(
                        self.geometry[0].at[place], self.x.at[side], self.xsem.at[2 * side]
                    ),
                    pltpu.make_async_copy(
                        self.geometry[1].at[place], self.s.at[side], self.xsem.at[2 * side + 1]
                    ),
                )
                for copy in copies:
                    copy.start()
                for copy in copies:
                    copy.wait()
            fill_factors(self.x[0], self.s[0], self.factors.at[0], self.factors.at[1])
            left = self.factors[0]
            fill_factors(self.x[1], self.s[1], self.factors.at[0], self.factors.at[1])
            self.ring[slot, k] = jnp.exp2(dot(left, self.factors[1], 0, 0)).astype(BF16)
            return carry

        lax.fori_loop(0, GROUP, one, 0)

    def run(self, vectors, offset, target):
        def step(t, carry):
            ahead = t + RING - 1

            @pl.when(self.stored(ahead))
            def _():
                self.read(ahead).start()

            have = self.stored(t)

            @pl.when(have)
            def _():
                self.read(t).wait()

            @pl.when(jnp.logical_not(have))
            def _():
                self.rebuild(t)

            slot = lax.rem(t, RING)
            for k in range(GROUP):
                row = self.tab[self.rows + t * GROUP + k]
                partner = self.tab[self.partners + t * GROUP + k] + offset
                target[row] += dot(vectors[partner], self.ring[slot, k], 1, 0)
            return carry

        lax.fori_loop(0, self.steps, step, 0)


def load_vectors(sz, tab, pieces, vbuf, sem):
    copies = []
    for s, piece in enumerate(pieces):
        if len(pieces) == 1:
            copies.append(pltpu.make_async_copy(piece, vbuf, sem.at[0]))
        else:
            owner = lax.rem(tab[sz.head] - s + sz.cols, sz.cols)
            copies.append(
                pltpu.make_async_copy(piece, vbuf.at[pl.ds(owner * sz.own, sz.own)], sem.at[s])
            )
    for copy in copies:
        copy.start()
    return copies


def sweep_cost(sz, entries):
    return pl.CostEstimate(
        flops=2 * entries * sz.width**2 * sz.vectors * 4,
        bytes_accessed=2 * entries * sz.width**2,
        transcendentals=0,
    )


def slot_products(sz, table, tiles, geometry, pieces, with_picks, kind):
    count = len(pieces)

    def kernel(tab, store, points, spreads, *refs):
        piece_refs, refs = refs[:count], refs[count:]
        out, refs = refs[0], refs[1:]
        if with_picks:
            picks, refs = refs[0], refs[1:]
        total, refs = refs[0], refs[1:]
        stream = Stream(sz, tab, "S", store, (points, spreads), refs)
        vbuf = refs[0]
        stream.begin()
        copies = load_vectors(sz, tab, piece_refs, vbuf, refs[3])
        total[...] = jnp.zeros(total.shape, F32)
        for copy in copies:
            copy.wait()
        if with_picks:
            for i in range(sz.slots):
                picks[i // sz.cap, i % sz.cap] = vbuf[jnp.minimum(tab[sz.mine + i], sz.blocks - 1)]
        stream.run(vbuf, 0, total)
        for i in range(sz.slots):
            out[i // sz.cap, i % sz.cap] = total[i].astype(kind)

    dims = (sz.peers, sz.cap, sz.vectors, sz.width)
    outs = (jax.ShapeDtypeStruct(dims, kind), jax.ShapeDtypeStruct(dims, BF16))
    outs = outs if with_picks else outs[:1]
    return pl.pallas_call(
        kernel,
        out_shape=outs,
        in_specs=[SMEM_SPEC] + [ANY_SPEC] * (3 + count),
        out_specs=(VMEM_SPEC,) * len(outs),
        scratch_shapes=[pltpu.VMEM((sz.slots + 1, sz.vectors, sz.width), F32)]
        + sweep_scratch(sz, sz.blocks),
        compiler_params=params(),
        cost_estimate=sweep_cost(sz, 12),
    )(table, tiles, *geometry, *pieces)


def local_products(sz, table, tiles, geometry, pieces):
    count = len(pieces)

    def kernel(tab, store, points, spreads, *refs):
        piece_refs, refs = refs[:count], refs[count:]
        out, total, refs = refs[0], refs[1], refs[2:]
        stream = Stream(sz, tab, "1", store, (points, spreads), refs)
        vbuf = refs[0]
        stream.begin()
        copies = load_vectors(sz, tab, piece_refs, vbuf, refs[3])
        total[...] = jnp.zeros(total.shape, F32)
        for copy in copies:
            copy.wait()
        stream.run(vbuf, 0, total)
        out[...] = total[0 : sz.own]

    return pl.pallas_call(
        kernel,
        out_shape=jax.ShapeDtypeStruct((sz.own, sz.vectors, sz.width), F32),
        in_specs=[SMEM_SPEC] + [ANY_SPEC] * (3 + count),
        out_specs=VMEM_SPEC,
        scratch_shapes=[pltpu.VMEM((sz.own + 1, sz.vectors, sz.width), F32)]
        + sweep_scratch(sz, sz.blocks),
        compiler_params=params(),
        cost_estimate=sweep_cost(sz, 64),
    )(table, tiles, *geometry, *pieces)


def far_products(sz, table, tiles, geometry, summed, far, returned, root, inverse):
    cells_total = sz.blocks * sz.width * sz.peers
    last = inverse is not None
    many = len(far)

    def kernel(tab, store, points, spreads, summed_ref, root_ref, *refs):
        if last:
            inverse_ref, refs = refs[0], refs[1:]
        far_refs, refs = refs[:many], refs[many:]
        back_refs, refs = refs[: sz.peers - 1], refs[sz.peers - 1 :]
        out, gram_out, total, refs = refs[0], refs[1], refs[2], refs[3:]
        stream = Stream(sz, tab, "2", store, (points, spreads), refs)
        vbuf, sem = refs[0], refs[3]
        stream.begin()
        if many == 1:
            copies = [pltpu.make_async_copy(far_refs[0], vbuf, sem.at[0])]
        else:
            copies = [
                pltpu.make_async_copy(far_refs[m - 1], vbuf.at[pl.ds(m * sz.cap, sz.cap)], sem.at[m])
                for m in range(1, sz.peers)
            ]
        for copy in copies:
            copy.start()
        z = tab[sz.head]
        total[0 : sz.own] = summed_ref[...]
        for m in range(1, sz.peers):
            for q in range(sz.cap):
                b = tab[sz.mine + m * sz.cap + q]
                place = jnp.where(b // sz.own == z, b - z * sz.own, sz.own)
                total[place] += back_refs[m - 1][q].astype(F32)
        for copy in copies:
            copy.wait()
        stream.run(vbuf, 0, total)
        gram = jnp.zeros((sz.vectors, sz.vectors), F32)
        for b in range(sz.own):
            root_row = root_ref[pl.ds(z * sz.own + b, 1), :]
            mapped = root_row * total[b]
            if last:
                mapped = dot(inverse_ref[...], mapped, 1, 0, lax.Precision.HIGHEST)
                out[b] = mapped
            else:
                out[b] = (root_row * mapped).astype(BF16)
            gram += dot(mapped, mapped, 1, 1, lax.Precision.HIGHEST)
        gram_out[...] = gram / cells_total

    args = [table, tiles, *geometry, summed, root]
    specs = [SMEM_SPEC] + [ANY_SPEC] * 3 + [VMEM_SPEC] * 2
    if last:
        args.append(inverse)
        specs.append(VMEM_SPEC)
    args += [*far, *returned]
    specs += [ANY_SPEC] * many + [VMEM_SPEC] * len(returned)
    return pl.pallas_call(
        kernel,
        out_shape=(
            jax.ShapeDtypeStruct((sz.own, sz.vectors, sz.width), F32 if last else BF16),
            jax.ShapeDtypeStruct((sz.vectors, sz.vectors), F32),
        ),
        in_specs=specs,
        out_specs=(VMEM_SPEC, VMEM_SPEC),
        scratch_shapes=[pltpu.VMEM((sz.own + 1, sz.vectors, sz.width), F32)]
        + sweep_scratch(sz, sz.slots),
        compiler_params=params(),
        cost_estimate=sweep_cost(sz, 20),
    )(*args)


def inverse_factor(gram):
    n = gram.shape[0]
    eye = (
        lax.broadcasted_iota(jnp.int32, (n, n), 0) == lax.broadcasted_iota(jnp.int32, (n, n), 1)
    ).astype(F32)
    whole = jnp.concatenate([gram, eye], axis=1)
    chunk = 8
    parts = [whole[i : i + chunk] for i in range(0, n, chunk)]
    row_ids = lax.broadcasted_iota(jnp.int32, (chunk, 1), 0)
    for k in range(n):
        at, inside = k // chunk, k % chunk
        row = parts[at][inside : inside + 1]
        pivot = row[:, k : k + 1]
        ratio = row / pivot
        for j in range(at, n // chunk):
            factor = parts[j][:, k : k + 1]
            if j == at:
                if inside == chunk - 1:
                    continue
                factor = jnp.where(row_ids > inside, factor, 0.0)
            parts[j] = parts[j] - factor * ratio
    out = []
    for j in range(n // chunk):
        diagonal = jnp.sum(
            parts[j][:, :n] * eye[j * chunk : (j + 1) * chunk], axis=1, keepdims=True
        )
        out.append(parts[j][:, n:] * lax.rsqrt(diagonal))
    return jnp.concatenate(out, axis=0)


def factor_call(sz, gram):
    def kernel(gram_ref, out):
        out[...] = inverse_factor(gram_ref[...])

    return pl.pallas_call(
        kernel,
        out_shape=jax.ShapeDtypeStruct((sz.vectors, sz.vectors), F32),
        in_specs=[VMEM_SPEC],
        out_specs=VMEM_SPEC,
    )(gram)


def normalize(sz, table, gram, mapped):
    share = sz.vectors // sz.cols

    def kernel(tab, gram_ref, mapped_ref, out, buf):
        inverse = inverse_factor(gram_ref[...])
        z = tab[sz.head]
        for b in range(sz.own):
            buf[...] = dot(inverse, mapped_ref[b], 1, 0, lax.Precision.HIGHEST)
            for s in range(sz.cols):
                to = lax.rem(z + s, sz.cols)
                out[s, b] = buf[pl.ds(pl.multiple_of(to * share, share), share)].astype(BF16)

    return pl.pallas_call(
        kernel,
        out_shape=jax.ShapeDtypeStruct((sz.cols, sz.own, share, sz.width), BF16),
        in_specs=[SMEM_SPEC, VMEM_SPEC, VMEM_SPEC],
        out_specs=VMEM_SPEC,
        scratch_shapes=[pltpu.VMEM((sz.vectors, sz.width), F32)],
        compiler_params=params(),
    )(table, gram, mapped)


def assemble(sz, table, pieces):
    share = sz.vectors // sz.cols

    def kernel(tab, *refs):
        out = refs[-1]
        z = tab[sz.head]
        for s in range(sz.cols):
            owner = lax.rem(z - s + sz.cols, sz.cols)
            for b in range(sz.own):
                out[owner * sz.own + b] = refs[s][b].astype(F32)

    return pl.pallas_call(
        kernel,
        out_shape=jax.ShapeDtypeStruct((sz.blocks, share, sz.width), F32),
        in_specs=[SMEM_SPEC] + [VMEM_SPEC] * sz.cols,
        out_specs=VMEM_SPEC,
        compiler_params=params(),
    )(table, *pieces)


def body(positions, scales, start_vectors, send_list, pair_rows, pair_partner):
    sz = Sizes(positions, start_vectors, send_list, pair_rows)
    c = lax.axis_index("cells")
    z = lax.axis_index("cols")
    where = jnp.stack([c, z]).astype(jnp.int32)

    pairs = jnp.concatenate([pair_rows.reshape(1, -1), pair_partner.reshape(1, -1)], axis=0)
    all_pairs = jnp.concatenate(spread(pairs, "cols"), axis=1)
    lists = send_list.reshape(1, -1)
    send_all = jnp.concatenate([lists] + exchange([lists] * sz.peers, "cells"), axis=0)

    relative = jnp.bitwise_xor(c, jnp.arange(sz.peers, dtype=jnp.int32))
    listed = jnp.take(send_list[0], relative, axis=0).reshape(-1)

    def pick(values):
        picked = jnp.take(values, listed, axis=0, mode="clip")
        return picked.reshape((sz.peers, sz.cap) + values.shape[1:])

    spreads = scales.astype(F32).reshape(sz.blocks, 1, sz.width)
    points_far = exchange(pick(positions), "cells")
    spreads_far = exchange(pick(spreads), "cells")
    start_far = exchange(pick(start_vectors), "cells")

    table = build_table(sz, all_pairs[0], all_pairs[1], send_all, where)
    tiles, sums = build_tiles(sz, table, ["1"], [positions], [spreads], None, None)
    tiles, sums = build_tiles(
        sz, table, ["S", "2"], [positions] + points_far, [spreads] + spreads_far, tiles, sums
    )
    geometry = (
        jnp.concatenate([positions, jnp.zeros_like(points_far[0])] + points_far, axis=0),
        jnp.concatenate([spreads, jnp.ones_like(spreads_far[0])] + spreads_far, axis=0),
    )

    column_sums = jnp.sum(sums, axis=1)
    owned = column_sums[: sz.own]
    slot_sums = column_sums[sz.own + 1 : sz.own + 1 + sz.slots]
    around = spread(jnp.concatenate([owned, slot_sums], axis=0), "cols")
    stacked = jnp.stack([piece[: sz.own] for piece in around])
    order = lax.rem(z - jnp.arange(sz.cols, dtype=jnp.int32) + sz.cols, sz.cols)
    group = jnp.take(stacked, order, axis=0).reshape(sz.blocks, sz.width)
    slot_total = sum(piece[sz.own :] for piece in around[1:]) + around[0][sz.own :]
    partial = jnp.concatenate([group, slot_total], axis=0)
    partials = [partial] + exchange([partial] * sz.peers, "cells")
    near, far, root = scale_start(sz, table, send_all, where, partials, start_vectors, start_far)

    (sent,) = slot_products(sz, table, tiles, geometry, [near], False, BF16)
    returned = exchange(sent, "cells")
    summed = local_products(sz, table, tiles, geometry, [near])
    scaled, gram = far_products(
        sz, table, tiles, geometry, summed, [far], returned, root, None
    )

    pieces = spread(scaled, "cols")
    gram = butterfly(butterfly(gram, "cells"), "cols")
    first_inverse = factor_call(sz, gram)
    sent, picks = slot_products(sz, table, tiles, geometry, pieces, True, F32)
    far_pieces = exchange(picks, "cells")
    returned = exchange(sent, "cells")
    summed = local_products(sz, table, tiles, geometry, pieces)
    mapped, gram = far_products(
        sz, table, tiles, geometry, summed, far_pieces, returned, root, first_inverse
    )
    gram = butterfly(butterfly(gram, "cells"), "cols")
    outgoing = normalize(sz, table, gram, mapped)
    n = sz.cols
    arrived = [outgoing[0]] + [
        lax.ppermute(outgoing[s], "cols", [(i, (i + s) % n) for i in range(n)]) for s in range(1, n)
    ]
    return assemble(sz, table, arrived)


def solution(mesh):
    in_specs = (
        P(("lineage", "cells"), None, None),
        P(("lineage", "cells"), None),
        P(("lineage", "cells"), None, None),
        P(("lineage", "cells"), None, None),
        P(("lineage", "cells"), "cols", None),
        P(("lineage", "cells"), "cols", None),
    )
    out_specs = P(("lineage", "cells"), "cols", None)
    return jax.shard_map(body, mesh=mesh, in_specs=in_specs, out_specs=out_specs, check_vma=False)
```

time: 802 us -> 246 us (0.31)
  other arithmetic: 215 us -> 6.82 us
  waiting for transfers between devices: 224 us -> 43.8 us
  matrix products: 156 us -> 0 us
  Pallas kernels: 0 us -> 126 us
  local copies, waits for them, and re-layouts: 95.4 us -> 23 us
  blocking collectives: 42.6 us -> 0 us
  loops' own time: 25.6 us -> 0 us
  starting transfers between devices: 26.5 us -> 42.7 us
  between operations: 13.8 us -> 0.71 us
    psum x2 -> x0, waiting for transfers between devices: 169 us -> none  [body(): summed = lax.psum(own_terms, 'cols')]
    dot_general x64 -> x0, matrix products: 156 us -> none  [the longest x24 56.5 us: vector_group(): jnp.einsum('gkj,gij->gki', far_vectors, kernel, preferred_element_type=jn...]
    scatter-add x75 -> x0, other arithmetic: 152 us -> none  [the longest x24 63.9 us: vector_group(): return running.at[partner_groups[group_index]].add(backward)]
    pallas_call x0 -> x13, Pallas kernels: none -> 126 us  [the longest x2 38 us: build_tiles(): pl.pallas_call(kernel, out_shape=(tile_shape, sum_shape), in_specs=specs,...]
    gather x125 -> x6, local copies, waits for them, and re-layouts: 71.9 us -> 5.33 us  [the longest x3 4.17 us: pick(): picked = jnp.take(values, listed, axis=0, mode='clip')]
    all_to_all x7 -> x0, waiting for transfers between devices: 54.8 us -> none  [the longest x2 25.6 us: body(): lax.all_to_all(partials[blocks:].reshape(peers, capacity, vector_count, w...]
    ppermute x0 -> x44, waiting for transfers between devices: none -> 43.8 us  [the longest x8 31.6 us: butterfly(): value = value + lax.ppermute(value, axis, [(i, i ^ step) for i in range(n)])]
    ppermute x0 -> x44, starting transfers between devices: none -> 42.7 us  [the longest x24 18.8 us: exchange(): lax.ppermute(pieces[m], axis, [(i, i ^ m) for i in range(n)])]
  transfers between devices with their start and end apart: 9 -> 44, of which waited for: 9 -> 17; matrix products, arithmetic and copies ran while one was open for 1% -> 7% of each run, Pallas kernels for 0% -> 33%
where the time goes in v1:
time: 246 us; the launch traced here: 244 us
  Pallas kernels  126 us (51%)
  waiting for transfers between devices  43.8 us (18%)
  starting transfers between devices  42.7 us (17%)
  local copies, waits for them, and re-layouts  23 us (9%)
  other arithmetic  6.82 us (3%)
    pallas_call x2, Pallas kernels, build_tiles(): pl.pallas_call(kernel, out_shape=(tile_shape, sum_shape), in_specs=specs,...  38 us
    ppermute x8, waiting for transfers between devices, butterfly(): value = value + lax.ppermute(value, axis, [(i, i ^ step) for i in range(n)])  31.6 us
    pallas_call x2, Pallas kernels, local_products(): pl.pallas_call(kernel, out_shape=jax.ShapeDtypeStruct((sz.own, sz.vectors...  28.6 us
    ppermute x24, starting transfers between devices, exchange(): lax.ppermute(pieces[m], axis, [(i, i ^ m) for i in range(n)])  18.8 us
    pallas_call x2, Pallas kernels, slot_products(): pl.pallas_call(kernel, out_shape=outs, in_specs=[SMEM_SPEC] + [ANY_SPEC]...  17.4 us
    ppermute x9, starting transfers between devices, spread(): lax.ppermute(value, axis, [(i, (i + s) % n) for i in range(n)])  15.5 us
    pallas_call x2, Pallas kernels, far_products(): pl.pallas_call(kernel, out_shape=(jax.ShapeDtypeStruct((sz.own, sz.vector...  15.1 us
    unnamed x75, local copies, waits for them, and re-layouts  8.81 us
  transfers between devices with their start and end apart: 44, of which 17 were waited for; matrix products, arithmetic and copies ran while one was open for 7% of the time, Pallas kernels for 33%

profile of v1, /device:TPU:0, one launch (start us, length us, event | category | flops | bytes accessed | tf_op | source)
XLA Modules:
  0.0 243.5 jit_solution(1374454248194846643)
XLA Ops:
  0.0 0.8 pad_add_fusion.2
  0.8 3.0 %collective-permute-start = (s32[2,48]{1,0:T(2,128)S(1)}, s32[2,48]{1,0:T(2,128)S(1)}, u32[]{:S(2)}, u32[]{:S(2)}) collective-permute-start(s32[2,48]{1,0:T(2,128)S(1)} %pad_add_fusion.2), channel_id=1, source_target_pairs={{0,1},{1,2},{2,3},{3,0},{4,5},{5,6},{6,7},{7,4},{8,9},{9,10},{10,1... | collective-permute-start | bytes 1160 | tf_op jit(solution)/shard_map/ppermute | solution.py:44
  3.8 2.6 %collective-permute-start.1 = (s32[2,48]{1,0:T(2,128)S(1)}, s32[2,48]{1,0:T(2,128)S(1)}, u32[]{:S(2)}, u32[]{:S(2)}) collective-permute-start(s32[2,48]{1,0:T(2,128)S(1)} %pad_add_fusion.2), channel_id=1, source_target_pairs={{0,2},{1,3},{2,0},{3,1},{4,6},{5,7},{6,4},{7,5},{8,10},{9,11},{10,... | collective-permute-start | bytes 1160 | tf_op jit(solution)/shard_map/ppermute | solution.py:44
  6.4 1.3 collective-permute-start.2
  7.7 0.8 copy.10
  8.6 1.6 collective-permute-start.4
  10.2 1.3 reshape.130.refs_2_.refs_5_
  11.5 0.7 reshape.129
  12.3 0.8 copy.11
  14.4 1.8 gather_fusion.1
  16.6 1.8 gather_fusion.4
  19.4 1.5 collective-permute-start.10
  20.9 1.2 collective-permute-done.5
  23.5 1.5 collective-permute-start.7
  25.6 8.1 %shard_map.64.refs_0_.tab = s32[1584]{0:T(1024)} custom-call(s32[192]{0:T(256)} %bitcast.47, s32[192]{0:T(256)} %bitcast.46, s32[4,8]{1,0:T(4,128)} %pad_add_fusion.1.send_ref, s32[2]{0:T(128)} %pad_add_fusion.3.where_ref), custom_call_target="tpu_custom_call" | custom-call | tf_op jit(solution)/shard_map/pallas_call | solution.py:136
  33.7 21.5 %shard_map.65 = (bf16[164,512,512]{2,1,0:T(8,128)(2,1)}, f32[14,8,512]{2,1,0:T(8,128)}) custom-call(s32[1584]{0:T(1024)} %shard_map.64.refs_0_.tab, bf16[16,64,512]{2,1,0:T(8,128)(2,1)} %refs_1_.3, f32[16,1,512]{2,1,0:T(1,128)} %reshape.130.refs_2_.refs_5_), custom_call_target="tpu_custom_call" | custom-call | flops 8589934592 | bytes 33554432 | tf_op jit(solution)/shard_map/pallas_call | solution.py:283
  55.2 2.4 collective-permute-start.8
  57.6 1.3 collective-permute-start.18
  59.0 1.4 collective-permute-start.20
  61.7 16.5 %shard_map.66 = (bf16[164,512,512]{2,1,0:T(8,128)(2,1)}, f32[14,8,512]{2,1,0:T(8,128)}) custom-call(s32[1584]{0:T(1024)} %shard_map.64.refs_0_.tab, bf16[16,64,512]{2,1,0:T(8,128)(2,1)} %refs_1_.3, bf16[2,64,512]{2,1,0:T(8,128)(2,1)} %copy-done.7, bf16[2,64,512]{2,1,0:T(8,128)(2,1)} %copy-done.8, ...), custom_call_target="tpu_custom_call", output_to_operand_aliasing={{0}: (9, {})} | custom-call | flops 3758096384 | bytes 14680064 | tf_op jit(solution)/shard_map/pallas_call | solution.py:283
  78.2 1.0 reduce_sum.9
  79.3 3.6 %collective-permute-start.13 = (f32[12,512]{1,0:T(8,128)S(1)}, f32[12,512]{1,0:T(8,128)S(1)}, u32[]{:S(2)}, u32[]{:S(2)}) collective-permute-start(f32[12,512]{1,0:T(8,128)S(1)} %pad_maximum_fusion.1), channel_id=1, source_target_pairs={{0,2},{1,3},{2,0},{3,1},{4,6},{5,7},{6,4},{7,5},{8,10},{9,11},{10,... | collective-permute-start | bytes 73736 | tf_op jit(solution)/shard_map/ppermute | solution.py:44
  82.9 0.9 constant_dynamic-update-slice_fusion.2
  83.9 0.9 constant_dynamic-update-slice_fusion.1
  84.8 1.0 collective-permute-start.12
  85.9 4.7 %collective-permute-done.12 = f32[12,512]{1,0:T(8,128)S(1)} collective-permute-done((f32[12,512]{1,0:T(8,128)S(1)}, f32[12,512]{1,0:T(8,128)S(1)}, u32[]{:S(2)}, u32[]{:S(2)}) %collective-permute-start.12) | collective-permute-done | bytes 24608 | tf_op jit(solution)/shard_map/ppermute | solution.py:44
  91.4 1.8 collective-permute-start.17
  93.2 0.9 constant_dynamic-update-slice_fusion.points
  94.2 1.8 collective-permute-done.16.refs_2_
  97.2 2.8 %shard_map.67 = (bf16[16,64,512]{2,1,0:T(8,128)(2,1)}, bf16[8,64,512]{2,1,0:T(8,128)(2,1)}, f32[16,512]{1,0:T(8,128)}) custom-call(s32[1584]{0:T(1024)} %shard_map.64.refs_0_.tab, s32[4,8]{1,0:T(4,128)} %pad_add_fusion.1.send_ref, s32[2]{0:T(128)} %pad_add_fusion.3.where_ref, f32[24,512]{1,0:T(8,128)} %copy-done.12, f32[24,512]{1,0:T(8,128)} %copy-done.25, ...), custom_call_target="tpu_custom_call" | custom-call | tf_op jit(solution)/shard_map/pallas_call | solution.py:332
  100.0 8.0 %shard_map.69 = bf16[4,2,64,512]{3,2,1,0:T(8,128)(2,1)} custom-call(s32[1584]{0:T(1024)} %shard_map.64.refs_0_.tab, bf16[164,512,512]{2,1,0:T(8,128)(2,1)} %get-tuple-element.20.store, bf16[24,64,512]{2,1,0:T(8,128)(2,1)} %copy-done, f32[24,1,512]{2,1,0:T(1,128)} %copy-done.2, bf16[16,64,512]{2,1,0:T(8,128)(2,1)} %get-tuple-element.22.refs_0_), custom_call_target="tpu_custom_call" | custom-call | flops 1610612736 | bytes 6291456 | tf_op jit(solution)/shard_map/pallas_call | solution.py:490
  108.0 1.1 slice_bitcast_fusion.3
  109.2 1.8 collective-permute-start.23
  111.0 14.3 %shard_map.68.summed_ref = f32[4,64,512]{2,1,0:T(8,128)} custom-call(s32[1584]{0:T(1024)} %shard_map.64.refs_0_.tab, bf16[164,512,512]{2,1,0:T(8,128)(2,1)} %get-tuple-element.20.store, bf16[24,64,512]{2,1,0:T(8,128)(2,1)} %copy-done, f32[24,1,512]{2,1,0:T(1,128)} %copy-done.2, bf16[16,64,512]{2,1,0:T(8,128)(2,1)} %get-tuple-element.22.refs_0_), custom_call_target="tpu_custom_call" | custom-call | flops 8589934592 | bytes 33554432 | tf_op jit(solution)/shard_map/pallas_call | solution.py:518
  126.2 6.8 %shard_map.70 = (bf16[4,64,512]{2,1,0:T(8,128)(2,1)}, f32[64,64]{1,0:T(8,128)}) custom-call(s32[1584]{0:T(1024)} %shard_map.64.refs_0_.tab, bf16[164,512,512]{2,1,0:T(8,128)(2,1)} %get-tuple-element.20.store, bf16[24,64,512]{2,1,0:T(8,128)(2,1)} %copy-done, f32[24,1,512]{2,1,0:T(1,128)} %copy-done.2, f32[4,64,512]{2,1,0:T(8,128)} %shard_map.68.summed_ref, ...), custom_call_target="tpu_custom_call" | custom-call | flops 2684354560 | bytes 10485760 | tf_op jit(solution)/shard_map/pallas_call | solution.py:582
  133.1 3.7 %collective-permute-start.26 = (bf16[4,64,512]{2,1,0:T(8,128)(2,1)}, bf16[4,64,512]{2,1,0:T(8,128)(2,1)S(1)}, u32[]{:S(2)}, u32[]{:S(2)}) collective-permute-start(bf16[4,64,512]{2,1,0:T(8,128)(2,1)} %get-tuple-element.25.refs_0_), channel_id=1, source_target_pairs={{0,3},{1,0},{2,1},{3,2},{4,7},{5,4},{6,5},{7,6},{8,11},{9,8},{10,9... | collective-permute-start | bytes 786440 | tf_op jit(solution)/shard_map/ppermute | solution.py:44
  136.8 1.4 collective-permute-done.27
  138.2 0.8 add.86
  139.0 1.3 collective-permute-start.28
  140.3 2.6 %collective-permute-done.28 = f32[64,64]{1,0:T(8,128)S(1)} collective-permute-done((f32[64,64]{1,0:T(8,128)S(1)}, f32[64,64]{1,0:T(8,128)S(1)}, u32[]{:S(2)}, u32[]{:S(2)}) %collective-permute-start.28) | collective-permute-done | bytes 16416 | tf_op jit(solution)/shard_map/ppermute | solution.py:52
  143.5 9.4 %collective-permute-done.29 = f32[64,64]{1,0:T(8,128)S(1)} collective-permute-done((f32[64,64]{1,0:T(8,128)S(1)}, f32[64,64]{1,0:T(8,128)S(1)}, u32[]{:S(2)}, u32[]{:S(2)}) %collective-permute-start.29) | collective-permute-done | bytes 16416 | tf_op jit(solution)/shard_map/ppermute | solution.py:52
  152.9 1.8 collective-permute-start.30
  154.8 4.9 %collective-permute-done.30 = f32[64,64]{1,0:T(8,128)S(1)} collective-permute-done((f32[64,64]{1,0:T(8,128)S(1)}, f32[64,64]{1,0:T(8,128)S(1)}, u32[]{:S(2)}, u32[]{:S(2)}) %collective-permute-start.30) | collective-permute-done | bytes 16416 | tf_op jit(solution)/shard_map/ppermute | solution.py:52
  160.3 6.8 %shard_map.72.refs_0_ = f32[64,64]{1,0:T(8,128)} custom-call(f32[64,64]{1,0:T(8,128)} %add.89.gram_ref), custom_call_target="tpu_custom_call" | custom-call | tf_op jit(solution)/shard_map/pallas_call | solution.py:631
  167.9 0.7 copy-done.5
  168.6 9.4 %shard_map.73 = (f32[4,2,64,512]{3,2,1,0:T(8,128)}, bf16[4,2,64,512]{3,2,1,0:T(8,128)(2,1)}) custom-call(s32[1584]{0:T(1024)} %shard_map.64.refs_0_.tab, bf16[164,512,512]{2,1,0:T(8,128)(2,1)} %get-tuple-element.20.store, bf16[24,64,512]{2,1,0:T(8,128)(2,1)} %copy-done, f32[24,1,512]{2,1,0:T(1,128)} %copy-done.2, ...), custom_call_target="tpu_custom_call" | custom-call | flops 1610612736 | bytes 6291456 | tf_op jit(solution)/shard_map/pallas_call | solution.py:490
  178.0 1.1 slice_bitcast_fusion.6
  179.2 1.2 slice_bitcast_fusion
  180.9 1.4 collective-permute-start.36
  183.0 1.4 collective-permute-start.33
  184.5 14.3 %shard_map.71.summed_ref = f32[4,64,512]{2,1,0:T(8,128)} custom-call(s32[1584]{0:T(1024)} %shard_map.64.refs_0_.tab, bf16[164,512,512]{2,1,0:T(8,128)(2,1)} %get-tuple-element.20.store, bf16[24,64,512]{2,1,0:T(8,128)(2,1)} %copy-done, f32[24,1,512]{2,1,0:T(1,128)} %copy-done.2, bf16[4,64,512]{2,1,0:T(8,128)(2,1)} %get-tuple-element.25.refs_0_, ...), custom_call_target="tpu_custom_call" | custom-call | flops 8589934592 | bytes 33554432 | tf_op jit(solution)/shard_map/pallas_call | solution.py:518
  198.8 0.8 collective-permute-done.33.refs_3_
  201.1 8.4 %shard_map.74 = (f32[4,64,512]{2,1,0:T(8,128)}, f32[64,64]{1,0:T(8,128)}) custom-call(s32[1584]{0:T(1024)} %shard_map.64.refs_0_.tab, bf16[164,512,512]{2,1,0:T(8,128)(2,1)} %get-tuple-element.20.store, bf16[24,64,512]{2,1,0:T(8,128)(2,1)} %copy-done, f32[24,1,512]{2,1,0:T(1,128)} %copy-done.2, f32[4,64,512]{2,1,0:T(8,128)} %shard_map.71.summed_ref, ...), custom_call_target="tpu_custom_call" | custom-call | flops 2684354560 | bytes 10485760 | tf_op jit(solution)/shard_map/pallas_call | solution.py:582
  209.7 1.3 collective-permute-done.37
  211.0 0.8 add.90
  211.8 0.7 collective-permute-start.38
  212.5 3.2 %collective-permute-done.38 = f32[64,64]{1,0:T(8,128)S(1)} collective-permute-done((f32[64,64]{1,0:T(8,128)S(1)}, f32[64,64]{1,0:T(8,128)S(1)}, u32[]{:S(2)}, u32[]{:S(2)}) %collective-permute-start.38) | collective-permute-done | bytes 16416 | tf_op jit(solution)/shard_map/ppermute | solution.py:52
  215.7 3.9 %collective-permute-done.39 = f32[64,64]{1,0:T(8,128)S(1)} collective-permute-done((f32[64,64]{1,0:T(8,128)S(1)}, f32[64,64]{1,0:T(8,128)S(1)}, u32[]{:S(2)}, u32[]{:S(2)}) %collective-permute-start.39) | collective-permute-done | bytes 16416 | tf_op jit(solution)/shard_map/ppermute | solution.py:52
  219.6 4.8 %collective-permute-done.40 = f32[64,64]{1,0:T(8,128)S(1)} collective-permute-done((f32[64,64]{1,0:T(8,128)S(1)}, f32[64,64]{1,0:T(8,128)S(1)}, u32[]{:S(2)}, u32[]{:S(2)}) %collective-permute-start.40) | collective-permute-done | bytes 16416 | tf_op jit(solution)/shard_map/ppermute | solution.py:52
  225.0 7.8 %shard_map.75 = bf16[4,4,16,512]{3,2,1,0:T(8,128)(2,1)} custom-call(s32[1584]{0:T(1024)} %shard_map.64.refs_0_.tab, f32[64,64]{1,0:T(8,128)} %add.93.gram_ref, f32[4,64,512]{2,1,0:T(8,128)} %get-tuple-element.30.mapped_ref), custom_call_target="tpu_custom_call" | custom-call | tf_op jit(solution)/shard_map/pallas_call | solution.py:651
  232.8 1.6 slice_bitcast_fusion.9
  234.4 3.8 %collective-permute-start.43 = (bf16[4,16,512]{2,1,0:T(8,128)(2,1)S(1)}, bf16[4,16,512]{2,1,0:T(8,128)(2,1)S(1)}, u32[]{:S(2)}, u32[]{:S(2)}) collective-permute-start(bf16[4,16,512]{2,1,0:T(8,128)(2,1)S(1)} %get-tuple-element.46), channel_id=1, source_target_pairs={{0,3},{1,0},{2,1},{3,2},{4,7},{5,4},{6,5},{7,6},{8,11},{9,8},{10,9... | collective-permute-start | bytes 196616 | tf_op jit(solution)/shard_map/ppermute | solution.py:747
  238.2 2.2 collective-permute-done.41.refs_1_
  241.7 1.8 shard_map.76
  (169 shorter events, 16.2 us)
Async XLA Ops:
  0.0 16.2 %copy-start.1 = (bf16[16,64,512]{2,1,0:T(8,128)(2,1)S(1)}, bf16[16,64,512]{2,1,0:T(8,128)(2,1)}, u32[]{:S(2)}) copy-start(bf16[16,64,512]{2,1,0:T(8,128)(2,1)} %refs_1_.3) | copy-start | bytes 3145732
  0.8 22.2 %collective-permute-start = (s32[2,48]{1,0:T(2,128)S(1)}, s32[2,48]{1,0:T(2,128)S(1)}, u32[]{:S(2)}, u32[]{:S(2)}) collective-permute-start(s32[2,48]{1,0:T(2,128)S(1)} %pad_add_fusion.2), channel_id=1, source_target_pairs={{0,1},{1,2},{2,3},{3,0},{4,5},{5,6},{6,7},{7,4},{8,9},{9,10},{10,1... | collective-permute-start | bytes 1160 | tf_op jit(solution)/shard_map/ppermute | solution.py:44
  3.8 19.5 %collective-permute-start.1 = (s32[2,48]{1,0:T(2,128)S(1)}, s32[2,48]{1,0:T(2,128)S(1)}, u32[]{:S(2)}, u32[]{:S(2)}) collective-permute-start(s32[2,48]{1,0:T(2,128)S(1)} %pad_add_fusion.2), channel_id=1, source_target_pairs={{0,2},{1,3},{2,0},{3,1},{4,6},{5,7},{6,4},{7,5},{8,10},{9,11},{10,... | collective-permute-start | bytes 1160 | tf_op jit(solution)/shard_map/ppermute | solution.py:44
  6.4 17.1 %collective-permute-start.2 = (s32[2,48]{1,0:T(2,128)S(1)}, s32[2,48]{1,0:T(2,128)S(1)}, u32[]{:S(2)}, u32[]{:S(2)}) collective-permute-start(s32[2,48]{1,0:T(2,128)S(1)} %pad_add_fusion.2), channel_id=1, source_target_pairs={{0,3},{1,0},{2,1},{3,2},{4,7},{5,4},{6,5},{7,6},{8,11},{9,8},{10,9... | collective-permute-start | bytes 1160 | tf_op jit(solution)/shard_map/ppermute | solution.py:44
  8.6 10.5 %collective-permute-start.3 = (s32[1,8]{1,0:T(1,128)S(1)}, s32[1,8]{1,0:T(1,128)S(1)}, u32[]{:S(2)}, u32[]{:S(2)}) collective-permute-start(s32[1,8]{1,0:T(1,128)S(1)} %reshape.126), channel_id=1, source_target_pairs={{0,4},{4,0},{8,12},{12,8},{1,5},{5,1},{9,13},{13,9},{2,6},{6,2},{1... | collective-permute-start | bytes 104 | tf_op jit(solution)/shard_map/ppermute | solution.py:37
  8.6 10.8 %collective-permute-start.4 = (s32[1,8]{1,0:T(1,128)S(1)}, s32[1,8]{1,0:T(1,128)S(1)}, u32[]{:S(2)}, u32[]{:S(2)}) collective-permute-start(s32[1,8]{1,0:T(1,128)S(1)} %reshape.126), channel_id=1, source_target_pairs={{0,8},{4,12},{8,0},{12,4},{1,9},{5,13},{9,1},{13,5},{2,10},{6,14},... | collective-permute-start | bytes 104 | tf_op jit(solution)/shard_map/ppermute | solution.py:37
  16.3 8.7 %copy-start.31 = (s32[1,1,48]{2,1,0:T(1,128)S(1)}, s32[1,1,48]{2,1,0:T(1,128)}, u32[]{:S(2)}) copy-start(s32[1,1,48]{2,1,0:T(1,128)} %param.11) | copy-start | bytes 580
  16.3 8.7 %copy-start.32 = (s32[1,1,48]{2,1,0:T(1,128)S(1)}, s32[1,1,48]{2,1,0:T(1,128)}, u32[]{:S(2)}) copy-start(s32[1,1,48]{2,1,0:T(1,128)} %param.10) | copy-start | bytes 580
  19.1 3.0 %collective-permute-start.5 = (s32[1,8]{1,0:T(1,128)S(1)}, s32[1,8]{1,0:T(1,128)S(1)}, u32[]{:S(2)}, u32[]{:S(2)}) collective-permute-start(s32[1,8]{1,0:T(1,128)S(1)} %reshape.126), channel_id=1, source_target_pairs={{0,12},{4,8},{8,4},{12,0},{1,13},{5,9},{9,5},{13,1},{2,14},{6,10},... | collective-permute-start | bytes 104 | tf_op jit(solution)/shard_map/ppermute | solution.py:37
  19.4 38.2 %collective-permute-start.10 = (f32[2,1,512]{2,1,0:T(1,128)S(1)}, f32[2,1,512]{2,1,0:T(1,128)S(1)}, u32[]{:S(2)}, u32[]{:S(2)}) collective-permute-start(f32[2,1,512]{2,1,0:T(1,128)S(1)} %reshape.177), channel_id=1, source_target_pairs={{0,8},{4,12},{8,0},{12,4},{1,9},{5,13},{9,1},{13,5},{2,10},{6,14},... | collective-permute-start | bytes 12296 | tf_op jit(solution)/shard_map/ppermute | solution.py:37
  22.1 36.9 %collective-permute-start.11 = (f32[2,1,512]{2,1,0:T(1,128)S(1)}, f32[2,1,512]{2,1,0:T(1,128)S(1)}, u32[]{:S(2)}, u32[]{:S(2)}) collective-permute-start(f32[2,1,512]{2,1,0:T(1,128)S(1)} %reshape.178), channel_id=1, source_target_pairs={{0,12},{4,8},{8,4},{12,0},{1,13},{5,9},{9,5},{13,1},{2,14},{6,10},... | collective-permute-start | bytes 12296 | tf_op jit(solution)/shard_map/ppermute | solution.py:37
  22.9 32.3 %collective-permute-start.9 = (f32[2,1,512]{2,1,0:T(1,128)S(1)}, f32[2,1,512]{2,1,0:T(1,128)S(1)}, u32[]{:S(2)}, u32[]{:S(2)}) collective-permute-start(f32[2,1,512]{2,1,0:T(1,128)S(1)} %reshape.176), channel_id=1, source_target_pairs={{0,4},{4,0},{8,12},{12,8},{1,5},{5,1},{9,13},{13,9},{2,6},{6,2},{1... | collective-permute-start | bytes 12296 | tf_op jit(solution)/shard_map/ppermute | solution.py:37
  23.3 35.7 %collective-permute-start.6 = (bf16[2,64,512]{2,1,0:T(8,128)(2,1)S(1)}, bf16[2,64,512]{2,1,0:T(8,128)(2,1)S(1)}, u32[]{:S(2)}, u32[]{:S(2)}) collective-permute-start(bf16[2,64,512]{2,1,0:T(8,128)(2,1)S(1)} %get-tuple-element.45), channel_id=1, source_target_pairs={{0,4},{4,0},{8,12},{12,8},{1,5},{5,1},{9,13},{13,9},{2,6},{6,2},{1... | collective-permute-start | bytes 393224 | tf_op jit(solution)/shard_map/ppermute | solution.py:37
  23.5 37.0 %collective-permute-start.7 = (bf16[2,64,512]{2,1,0:T(8,128)(2,1)S(1)}, bf16[2,64,512]{2,1,0:T(8,128)(2,1)S(1)}, u32[]{:S(2)}, u32[]{:S(2)}) collective-permute-start(bf16[2,64,512]{2,1,0:T(8,128)(2,1)S(1)} %get-tuple-element.44), channel_id=1, source_target_pairs={{0,8},{4,12},{8,0},{12,4},{1,9},{5,13},{9,1},{13,5},{2,10},{6,14},... | collective-permute-start | bytes 393224 | tf_op jit(solution)/shard_map/ppermute | solution.py:37
  55.2 5.8 %copy-start.30 = (f32[2,1,512]{2,1,0:T(1,128)}, f32[2,1,512]{2,1,0:T(1,128)S(1)}, u32[]{:S(2)}) copy-start(f32[2,1,512]{2,1,0:T(1,128)S(1)} %collective-permute-done.9.refs_6_) | copy-start | bytes 12292
  55.2 5.8 %collective-permute-start.8 = (bf16[2,64,512]{2,1,0:T(8,128)(2,1)S(1)}, bf16[2,64,512]{2,1,0:T(8,128)(2,1)S(1)}, u32[]{:S(2)}, u32[]{:S(2)}) collective-permute-start(bf16[2,64,512]{2,1,0:T(8,128)(2,1)S(1)} %get-tuple-element.43), channel_id=1, source_target_pairs={{0,12},{4,8},{8,4},{12,0},{1,13},{5,9},{9,5},{13,1},{2,14},{6,10},... | collective-permute-start | bytes 393224 | tf_op jit(solution)/shard_map/ppermute | solution.py:37
  57.6 3.4 %copy-start.28 = (f32[2,1,512]{2,1,0:T(1,128)}, f32[2,1,512]{2,1,0:T(1,128)S(1)}, u32[]{:S(2)}) copy-start(f32[2,1,512]{2,1,0:T(1,128)S(1)} %collective-permute-done.10.refs_7_) | copy-start | bytes 12292
  57.6 33.8 %collective-permute-start.18 = (bf16[2,64,512]{2,1,0:T(8,128)(2,1)S(1)}, bf16[2,64,512]{2,1,0:T(8,128)(2,1)S(1)}, u32[]{:S(2)}, u32[]{:S(2)}) collective-permute-start(bf16[2,64,512]{2,1,0:T(8,128)(2,1)S(1)} %get-tuple-element.42), channel_id=1, source_target_pairs={{0,4},{4,0},{8,12},{12,8},{1,5},{5,1},{9,13},{13,9},{2,6},{6,2},{1... | collective-permute-start | bytes 393224 | tf_op jit(solution)/shard_map/ppermute | solution.py:37
  58.9 2.1 copy-start.29
  58.9 35.2 %collective-permute-start.19 = (bf16[2,64,512]{2,1,0:T(8,128)(2,1)S(1)}, bf16[2,64,512]{2,1,0:T(8,128)(2,1)S(1)}, u32[]{:S(2)}, u32[]{:S(2)}) collective-permute-start(bf16[2,64,512]{2,1,0:T(8,128)(2,1)S(1)} %get-tuple-element.41), channel_id=1, source_target_pairs={{0,8},{4,12},{8,0},{12,4},{1,9},{5,13},{9,1},{13,5},{2,10},{6,14},... | collective-permute-start | bytes 393224 | tf_op jit(solution)/shard_map/ppermute | solution.py:37
  59.0 19.2 %copy-start.2 = (f32[24,1,512]{2,1,0:T(1,128)}, f32[24,1,512]{2,1,0:T(1,128)S(1)}, u32[]{:S(2)}) copy-start(f32[24,1,512]{2,1,0:T(1,128)S(1)} %constant_dynamic-update-slice_fusion.4.spreads) | copy-start | bytes 147460
  59.0 2.0 copy-start.7
  59.0 35.1 %collective-permute-start.20 = (bf16[2,64,512]{2,1,0:T(8,128)(2,1)S(1)}, bf16[2,64,512]{2,1,0:T(8,128)(2,1)S(1)}, u32[]{:S(2)}, u32[]{:S(2)}) collective-permute-start(bf16[2,64,512]{2,1,0:T(8,128)(2,1)S(1)} %get-tuple-element.40), channel_id=1, source_target_pairs={{0,12},{4,8},{8,4},{12,0},{1,13},{5,9},{9,5},{13,1},{2,14},{6,10},... | collective-permute-start | bytes 393224 | tf_op jit(solution)/shard_map/ppermute | solution.py:37
  79.2 5.5 %collective-permute-start.14 = (f32[12,512]{1,0:T(8,128)S(1)}, f32[12,512]{1,0:T(8,128)S(1)}, u32[]{:S(2)}, u32[]{:S(2)}) collective-permute-start(f32[12,512]{1,0:T(8,128)S(1)} %pad_maximum_fusion.1), channel_id=1, source_target_pairs={{0,3},{1,0},{2,1},{3,2},{4,7},{5,4},{6,5},{7,6},{8,11},{9,8},{10,9... | collective-permute-start | bytes 73736 | tf_op jit(solution)/shard_map/ppermute | solution.py:44
  79.3 6.6 %collective-permute-start.13 = (f32[12,512]{1,0:T(8,128)S(1)}, f32[12,512]{1,0:T(8,128)S(1)}, u32[]{:S(2)}, u32[]{:S(2)}) collective-permute-start(f32[12,512]{1,0:T(8,128)S(1)} %pad_maximum_fusion.1), channel_id=1, source_target_pairs={{0,2},{1,3},{2,0},{3,1},{4,6},{5,7},{6,4},{7,5},{8,10},{9,11},{10,... | collective-permute-start | bytes 73736 | tf_op jit(solution)/shard_map/ppermute | solution.py:44
  84.8 5.8 %collective-permute-start.12 = (f32[12,512]{1,0:T(8,128)S(1)}, f32[12,512]{1,0:T(8,128)S(1)}, u32[]{:S(2)}, u32[]{:S(2)}) collective-permute-start(f32[12,512]{1,0:T(8,128)S(1)} %pad_maximum_fusion.1), channel_id=1, source_target_pairs={{0,1},{1,2},{2,3},{3,0},{4,5},{5,6},{6,7},{7,4},{8,9},{9,10},{10,1... | collective-permute-start | bytes 73736 | tf_op jit(solution)/shard_map/ppermute | solution.py:44
  91.3 4.8 %copy-start.12 = (f32[24,512]{1,0:T(8,128)}, f32[24,512]{1,0:T(8,128)S(1)}, u32[]{:S(2)}) copy-start(f32[24,512]{1,0:T(8,128)S(1)} %pad_maximum_fusion.refs_0_) | copy-start | bytes 147460
  91.3 2.9 %collective-permute-start.15 = (f32[24,512]{1,0:T(8,128)S(1)}, f32[24,512]{1,0:T(8,128)S(1)}, u32[]{:S(2)}, u32[]{:S(2)}) collective-permute-start(f32[24,512]{1,0:T(8,128)S(1)} %pad_maximum_fusion.refs_0_), channel_id=1, source_target_pairs={{0,4},{4,0},{8,12},{12,8},{1,5},{5,1},{9,13},{13,9},{2,6},{6,2},{1... | collective-permute-start | bytes 147464 | tf_op jit(solution)/shard_map/ppermute | solution.py:37
  91.3 4.6 %collective-permute-start.16 = (f32[24,512]{1,0:T(8,128)S(1)}, f32[24,512]{1,0:T(8,128)S(1)}, u32[]{:S(2)}, u32[]{:S(2)}) collective-permute-start(f32[24,512]{1,0:T(8,128)S(1)} %pad_maximum_fusion.refs_0_), channel_id=1, source_target_pairs={{0,8},{4,12},{8,0},{12,4},{1,9},{5,13},{9,1},{13,5},{2,10},{6,14},... | collective-permute-start | bytes 147464 | tf_op jit(solution)/shard_map/ppermute | solution.py:37
  91.4 4.7 %copy-start.19 = (bf16[2,64,512]{2,1,0:T(8,128)(2,1)}, bf16[2,64,512]{2,1,0:T(8,128)(2,1)S(1)}, u32[]{:S(2)}) copy-start(bf16[2,64,512]{2,1,0:T(8,128)(2,1)S(1)} %collective-permute-done.18.refs_5_) | copy-start | bytes 393220
  91.4 4.7 %collective-permute-start.17 = (f32[24,512]{1,0:T(8,128)S(1)}, f32[24,512]{1,0:T(8,128)S(1)}, u32[]{:S(2)}, u32[]{:S(2)}) collective-permute-start(f32[24,512]{1,0:T(8,128)S(1)} %pad_maximum_fusion.refs_0_), channel_id=1, source_target_pairs={{0,12},{4,8},{8,4},{12,0},{1,13},{5,9},{9,5},{13,1},{2,14},{6,10},... | collective-permute-start | bytes 147464 | tf_op jit(solution)/shard_map/ppermute | solution.py:37
  94.1 5.9 %copy-start = (bf16[24,64,512]{2,1,0:T(8,128)(2,1)}, bf16[24,64,512]{2,1,0:T(8,128)(2,1)S(1)}, u32[]{:S(2)}) copy-start(bf16[24,64,512]{2,1,0:T(8,128)(2,1)S(1)} %constant_dynamic-update-slice_fusion.points) | copy-start | bytes 4718596
  94.2 2.0 copy-start.20
  94.2 1.9 copy-start.21
  94.2 1.9 copy-start.25
  109.1 16.3 %collective-permute-start.21 = (bf16[2,64,512]{2,1,0:T(8,128)(2,1)S(1)}, bf16[2,64,512]{2,1,0:T(8,128)(2,1)S(1)}, u32[]{:S(2)}, u32[]{:S(2)}) collective-permute-start(bf16[2,64,512]{2,1,0:T(8,128)(2,1)S(1)} %get-tuple-element.39), channel_id=1, source_target_pairs={{0,4},{4,0},{8,12},{12,8},{1,5},{5,1},{9,13},{13,9},{2,6},{6,2},{1... | collective-permute-start | bytes 393224 | tf_op jit(solution)/shard_map/ppermute | solution.py:37
  109.2 16.2 %collective-permute-start.22 = (bf16[2,64,512]{2,1,0:T(8,128)(2,1)S(1)}, bf16[2,64,512]{2,1,0:T(8,128)(2,1)S(1)}, u32[]{:S(2)}, u32[]{:S(2)}) collective-permute-start(bf16[2,64,512]{2,1,0:T(8,128)(2,1)S(1)} %get-tuple-element.38), channel_id=1, source_target_pairs={{0,8},{4,12},{8,0},{12,4},{1,9},{5,13},{9,1},{13,5},{2,10},{6,14},... | collective-permute-start | bytes 393224 | tf_op jit(solution)/shard_map/ppermute | solution.py:37
  109.2 16.2 %collective-permute-start.23 = (bf16[2,64,512]{2,1,0:T(8,128)(2,1)S(1)}, bf16[2,64,512]{2,1,0:T(8,128)(2,1)S(1)}, u32[]{:S(2)}, u32[]{:S(2)}) collective-permute-start(bf16[2,64,512]{2,1,0:T(8,128)(2,1)S(1)} %get-tuple-element.37), channel_id=1, source_target_pairs={{0,12},{4,8},{8,4},{12,0},{1,13},{5,9},{9,5},{13,1},{2,14},{6,10},... | collective-permute-start | bytes 393224 | tf_op jit(solution)/shard_map/ppermute | solution.py:37
  125.4 0.7 copy-start.18
  132.9 34.2 %collective-permute-start.24 = (bf16[4,64,512]{2,1,0:T(8,128)(2,1)}, bf16[4,64,512]{2,1,0:T(8,128)(2,1)S(1)}, u32[]{:S(2)}, u32[]{:S(2)}) collective-permute-start(bf16[4,64,512]{2,1,0:T(8,128)(2,1)} %get-tuple-element.25.refs_0_), channel_id=1, source_target_pairs={{0,1},{1,2},{2,3},{3,0},{4,5},{5,6},{6,7},{7,4},{8,9},{9,10},{10,1... | collective-permute-start | bytes 786440 | tf_op jit(solution)/shard_map/ppermute | solution.py:44
  133.0 34.1 %collective-permute-start.25 = (bf16[4,64,512]{2,1,0:T(8,128)(2,1)}, bf16[4,64,512]{2,1,0:T(8,128)(2,1)S(1)}, u32[]{:S(2)}, u32[]{:S(2)}) collective-permute-start(bf16[4,64,512]{2,1,0:T(8,128)(2,1)} %get-tuple-element.25.refs_0_), channel_id=1, source_target_pairs={{0,2},{1,3},{2,0},{3,1},{4,6},{5,7},{6,4},{7,5},{8,10},{9,11},{10,... | collective-permute-start | bytes 786440 | tf_op jit(solution)/shard_map/ppermute | solution.py:44
  133.1 34.0 %collective-permute-start.26 = (bf16[4,64,512]{2,1,0:T(8,128)(2,1)}, bf16[4,64,512]{2,1,0:T(8,128)(2,1)S(1)}, u32[]{:S(2)}, u32[]{:S(2)}) collective-permute-start(bf16[4,64,512]{2,1,0:T(8,128)(2,1)} %get-tuple-element.25.refs_0_), channel_id=1, source_target_pairs={{0,3},{1,0},{2,1},{3,2},{4,7},{5,4},{6,5},{7,6},{8,11},{9,8},{10,9... | collective-permute-start | bytes 786440 | tf_op jit(solution)/shard_map/ppermute | solution.py:44
  136.8 1.4 collective-permute-start.27
  139.0 3.9 %collective-permute-start.28 = (f32[64,64]{1,0:T(8,128)S(1)}, f32[64,64]{1,0:T(8,128)S(1)}, u32[]{:S(2)}, u32[]{:S(2)}) collective-permute-start(f32[64,64]{1,0:T(8,128)S(1)} %add.86), channel_id=1, source_target_pairs={{0,8},{4,12},{8,0},{12,4},{1,9},{5,13},{9,1},{13,5},{2,10},{6,14},... | collective-permute-start | bytes 49160 | tf_op jit(solution)/shard_map/ppermute | solution.py:52
  142.9 10.0 %collective-permute-start.29 = (f32[64,64]{1,0:T(8,128)S(1)}, f32[64,64]{1,0:T(8,128)S(1)}, u32[]{:S(2)}, u32[]{:S(2)}) collective-permute-start(f32[64,64]{1,0:T(8,128)S(1)} %add.87), channel_id=1, source_target_pairs={{0,1},{1,0},{2,3},{3,2},{4,5},{5,4},{6,7},{7,6},{8,9},{9,8},{10,11... | collective-permute-start | bytes 49160 | tf_op jit(solution)/shard_map/ppermute | solution.py:52
  152.9 6.8 %collective-permute-start.30 = (f32[64,64]{1,0:T(8,128)S(1)}, f32[64,64]{1,0:T(8,128)S(1)}, u32[]{:S(2)}, u32[]{:S(2)}) collective-permute-start(f32[64,64]{1,0:T(8,128)S(1)} %add.88), channel_id=1, source_target_pairs={{0,2},{1,3},{2,0},{3,1},{4,6},{5,7},{6,4},{7,5},{8,10},{9,11},{10,... | collective-permute-start | bytes 49160 | tf_op jit(solution)/shard_map/ppermute | solution.py:52
  167.1 0.8 copy-start.4
  179.1 3.9 %collective-permute-start.31 = (bf16[2,64,512]{2,1,0:T(8,128)(2,1)S(1)}, bf16[2,64,512]{2,1,0:T(8,128)(2,1)S(1)}, u32[]{:S(2)}, u32[]{:S(2)}) collective-permute-start(bf16[2,64,512]{2,1,0:T(8,128)(2,1)S(1)} %get-tuple-element.36), channel_id=1, source_target_pairs={{0,4},{4,0},{8,12},{12,8},{1,5},{5,1},{9,13},{13,9},{2,6},{6,2},{1... | collective-permute-start | bytes 393224 | tf_op jit(solution)/shard_map/ppermute | solution.py:37
  180.4 19.2 %collective-permute-start.34 = (f32[2,64,512]{2,1,0:T(8,128)S(1)}, f32[2,64,512]{2,1,0:T(8,128)S(1)}, u32[]{:S(2)}, u32[]{:S(2)}) collective-permute-start(f32[2,64,512]{2,1,0:T(8,128)S(1)} %get-tuple-element.33), channel_id=1, source_target_pairs={{0,4},{4,0},{8,12},{12,8},{1,5},{5,1},{9,13},{13,9},{2,6},{6,2},{1... | collective-permute-start | bytes 786440 | tf_op jit(solution)/shard_map/ppermute | solution.py:37
  180.9 18.7 %collective-permute-start.35 = (f32[2,64,512]{2,1,0:T(8,128)S(1)}, f32[2,64,512]{2,1,0:T(8,128)S(1)}, u32[]{:S(2)}, u32[]{:S(2)}) collective-permute-start(f32[2,64,512]{2,1,0:T(8,128)S(1)} %get-tuple-element.32), channel_id=1, source_target_pairs={{0,8},{4,12},{8,0},{12,4},{1,9},{5,13},{9,1},{13,5},{2,10},{6,14},... | collective-permute-start | bytes 786440 | tf_op jit(solution)/shard_map/ppermute | solution.py:37
  180.9 18.7 %collective-permute-start.36 = (f32[2,64,512]{2,1,0:T(8,128)S(1)}, f32[2,64,512]{2,1,0:T(8,128)S(1)}, u32[]{:S(2)}, u32[]{:S(2)}) collective-permute-start(f32[2,64,512]{2,1,0:T(8,128)S(1)} %get-tuple-element.31), channel_id=1, source_target_pairs={{0,12},{4,8},{8,4},{12,0},{1,13},{5,9},{9,5},{13,1},{2,14},{6,10},... | collective-permute-start | bytes 786440 | tf_op jit(solution)/shard_map/ppermute | solution.py:37
  182.4 16.4 %collective-permute-start.32 = (bf16[2,64,512]{2,1,0:T(8,128)(2,1)S(1)}, bf16[2,64,512]{2,1,0:T(8,128)(2,1)S(1)}, u32[]{:S(2)}, u32[]{:S(2)}) collective-permute-start(bf16[2,64,512]{2,1,0:T(8,128)(2,1)S(1)} %get-tuple-element.35), channel_id=1, source_target_pairs={{0,8},{4,12},{8,0},{12,4},{1,9},{5,13},{9,1},{13,5},{2,10},{6,14},... | collective-permute-start | bytes 393224 | tf_op jit(solution)/shard_map/ppermute | solution.py:37
  183.0 15.8 %copy-start.13 = (bf16[2,64,512]{2,1,0:T(8,128)(2,1)}, bf16[2,64,512]{2,1,0:T(8,128)(2,1)S(1)}, u32[]{:S(2)}) copy-start(bf16[2,64,512]{2,1,0:T(8,128)(2,1)S(1)} %collective-permute-done.31.refs_1_) | copy-start | bytes 393220
  183.0 16.6 %collective-permute-start.33 = (bf16[2,64,512]{2,1,0:T(8,128)(2,1)S(1)}, bf16[2,64,512]{2,1,0:T(8,128)(2,1)S(1)}, u32[]{:S(2)}, u32[]{:S(2)}) collective-permute-start(bf16[2,64,512]{2,1,0:T(8,128)(2,1)S(1)} %get-tuple-element.34), channel_id=1, source_target_pairs={{0,12},{4,8},{8,4},{12,0},{1,13},{5,9},{9,5},{13,1},{2,14},{6,10},... | collective-permute-start | bytes 393224 | tf_op jit(solution)/shard_map/ppermute | solution.py:37
  198.8 0.9 copy-start.14
  199.6 0.8 copy-start.9
  199.6 0.9 copy-start.10
  209.5 1.5 collective-permute-start.37
  211.8 3.9 %collective-permute-start.38 = (f32[64,64]{1,0:T(8,128)S(1)}, f32[64,64]{1,0:T(8,128)S(1)}, u32[]{:S(2)}, u32[]{:S(2)}) collective-permute-start(f32[64,64]{1,0:T(8,128)S(1)} %add.90), channel_id=1, source_target_pairs={{0,8},{4,12},{8,0},{12,4},{1,9},{5,13},{9,1},{13,5},{2,10},{6,14},... | collective-permute-start | bytes 49160 | tf_op jit(solution)/shard_map/ppermute | solution.py:52
  215.7 3.9 %collective-permute-start.39 = (f32[64,64]{1,0:T(8,128)S(1)}, f32[64,64]{1,0:T(8,128)S(1)}, u32[]{:S(2)}, u32[]{:S(2)}) collective-permute-start(f32[64,64]{1,0:T(8,128)S(1)} %add.91), channel_id=1, source_target_pairs={{0,1},{1,0},{2,3},{3,2},{4,5},{5,4},{6,7},{7,6},{8,9},{9,8},{10,11... | collective-permute-start | bytes 49160 | tf_op jit(solution)/shard_map/ppermute | solution.py:52
  219.6 4.8 %collective-permute-start.40 = (f32[64,64]{1,0:T(8,128)S(1)}, f32[64,64]{1,0:T(8,128)S(1)}, u32[]{:S(2)}, u32[]{:S(2)}) collective-permute-start(f32[64,64]{1,0:T(8,128)S(1)} %add.92), channel_id=1, source_target_pairs={{0,2},{1,3},{2,0},{3,1},{4,6},{5,7},{6,4},{7,5},{8,10},{9,11},{10,... | collective-permute-start | bytes 49160 | tf_op jit(solution)/shard_map/ppermute | solution.py:52
  234.3 6.1 %collective-permute-start.41 = (bf16[4,16,512]{2,1,0:T(8,128)(2,1)S(1)}, bf16[4,16,512]{2,1,0:T(8,128)(2,1)S(1)}, u32[]{:S(2)}, u32[]{:S(2)}) collective-permute-start(bf16[4,16,512]{2,1,0:T(8,128)(2,1)S(1)} %get-tuple-element.48), channel_id=1, source_target_pairs={{0,1},{1,2},{2,3},{3,0},{4,5},{5,6},{6,7},{7,4},{8,9},{9,10},{10,1... | collective-permute-start | bytes 196616 | tf_op jit(solution)/shard_map/ppermute | solution.py:747
  234.4 6.1 %collective-permute-start.42 = (bf16[4,16,512]{2,1,0:T(8,128)(2,1)S(1)}, bf16[4,16,512]{2,1,0:T(8,128)(2,1)S(1)}, u32[]{:S(2)}, u32[]{:S(2)}) collective-permute-start(bf16[4,16,512]{2,1,0:T(8,128)(2,1)S(1)} %get-tuple-element.47), channel_id=1, source_target_pairs={{0,2},{1,3},{2,0},{3,1},{4,6},{5,7},{6,4},{7,5},{8,10},{9,11},{10,... | collective-permute-start | bytes 196616 | tf_op jit(solution)/shard_map/ppermute | solution.py:747
  234.4 6.7 %collective-permute-start.43 = (bf16[4,16,512]{2,1,0:T(8,128)(2,1)S(1)}, bf16[4,16,512]{2,1,0:T(8,128)(2,1)S(1)}, u32[]{:S(2)}, u32[]{:S(2)}) collective-permute-start(bf16[4,16,512]{2,1,0:T(8,128)(2,1)S(1)} %get-tuple-element.46), channel_id=1, source_target_pairs={{0,3},{1,0},{2,1},{3,2},{4,7},{5,4},{6,5},{7,6},{8,11},{9,8},{10,9... | collective-permute-start | bytes 196616 | tf_op jit(solution)/shard_map/ppermute | solution.py:747
  (13 other events, 8.6 us)

commit v2 on v1

v2 whole, which is shorter than its diff:
```python
import math

import jax
import jax.numpy as jnp
from jax import lax
from jax.experimental import pallas as pl
from jax.experimental.pallas import tpu as pltpu
from jax.sharding import PartitionSpec as P

F32 = jnp.float32
BF16 = jnp.bfloat16
LOG2E = math.log2(math.e)
GROUP = 4
RING = 4
STORED = 160
DEPTH = 256
VMEM_BYTES = 56 * 2**20

VMEM_SPEC = pl.BlockSpec(memory_space=pltpu.VMEM)
SMEM_SPEC = pl.BlockSpec(memory_space=pltpu.SMEM)
ANY_SPEC = pl.BlockSpec(memory_space=pl.ANY)


def dot(a, b, ca, cb, precision=None):
    return lax.dot_general(
        a, b, (((ca,), (cb,)), ((), ())), preferred_element_type=F32, precision=precision
    )


def params():
    return pltpu.CompilerParams(vmem_limit_bytes=VMEM_BYTES)


def exchange(pieces, axis):
    n = lax.axis_size(axis)
    return [
        lax.ppermute(pieces[m], axis, [(i, i ^ m) for i in range(n)]) for m in range(1, n)
    ]


def spread(value, axis):
    n = lax.axis_size(axis)
    return [value] + [
        lax.ppermute(value, axis, [(i, (i + s) % n) for i in range(n)]) for s in range(1, n)
    ]


def butterfly(value, axis):
    n = lax.axis_size(axis)
    step = 1
    while step < n:
        value = value + lax.ppermute(value, axis, [(i, i ^ step) for i in range(n)])
        step *= 2
    return value


class Sizes:
    def __init__(self, positions, start, send_list, pair_rows):
        self.blocks, self.comps, self.width = positions.shape
        self.vectors = start.shape[1]
        self.peers = lax.axis_size("cells")
        self.cols = lax.axis_size("cols")
        self.cap = send_list.shape[2]
        self.slots = self.peers * self.cap
        self.own = self.blocks // self.cols
        self.pairs = pair_rows.shape[2] * self.cols
        self.long = 2 * self.pairs + GROUP
        self.short = self.pairs + GROUP
        self.at0, self.at1 = 0, self.long
        self.ats = 2 * self.long
        self.at2 = self.ats + self.short
        self.head = self.at2 + self.short
        self.mine = self.head + 8
        self.theirs = self.mine + self.slots
        self.table = self.theirs + self.slots
        self.bundle = self.comps + self.vectors + 16


def divide(value, by):
    if by & (by - 1):
        return value // by
    return lax.shift_right_arithmetic(value, jnp.int32(by.bit_length() - 1))


def remainder(value, by):
    if by & (by - 1):
        return value % by
    return jnp.bitwise_and(value, jnp.int32(by - 1))


def build_table(sz, pairs, send_all, where):
    count = len(pairs)
    each = sz.pairs // sz.cols

    def kernel(*refs):
        pair_refs, (send_ref, where_ref, tab, slot_owner) = refs[:count], refs[count:]
        c = where_ref[0]
        z = where_ref[1]
        base = z * sz.own

        def lists(i, carry):
            m = divide(i, sz.cap)
            q = remainder(i, sz.cap)
            tab[sz.mine + i] = send_ref[0, jnp.bitwise_xor(c, m) * sz.cap + q]
            tab[sz.theirs + i] = send_ref[m, c * sz.cap + q]
            slot_owner[i] = divide(send_ref[m, c * sz.cap + q], sz.own)
            return carry

        lax.fori_loop(0, sz.slots, lists, 0)
        carry = (jnp.int32(0),) * 4
        for ref in pair_refs:

            def pair(i, carry, ref=ref):
                n0, n1, ns, n2 = carry
                r = ref[0, i]
                p = ref[1, i]
                local = p < sz.blocks
                row_mine = divide(r, sz.own) == z
                partner_mine = divide(p, sz.own) == z
                slot = jnp.maximum(p - sz.blocks, 0)
                slot = jnp.bitwise_xor(divide(slot, sz.cap), c) * sz.cap + remainder(slot, sz.cap)
                slot_mine = slot_owner[slot] == z
                forward = (r - base) * 256 + p
                back = (p - base) * 256 + r
                both = jnp.logical_and(row_mine, partner_mine)
                other = jnp.logical_and(local, row_mine != partner_mine)
                tab[sz.at0 + n0] = forward
                n0 = n0 + jnp.where(both, 1, 0)
                tab[sz.at0 + n0] = back
                n0 = n0 + jnp.where(jnp.logical_and(both, p != r), 1, 0)
                tab[sz.at1 + n1] = jnp.where(row_mine, forward, back)
                n1 = n1 + jnp.where(other, 1, 0)
                far = jnp.logical_not(local)
                tab[sz.at2 + n2] = (r - base) * 256 + slot
                n2 = n2 + jnp.where(jnp.logical_and(far, row_mine), 1, 0)
                tab[sz.ats + ns] = slot * 256 + r
                ns = ns + jnp.where(jnp.logical_and(far, slot_mine), 1, 0)
                return n0, n1, ns, n2

            carry = lax.fori_loop(0, each, pair, carry, unroll=4)
        n0, n1, ns, n2 = carry
        tab[sz.head] = z
        for k, (at, n, dummy) in enumerate(
            ((sz.at0, n0, sz.own), (sz.at1, n1, sz.own), (sz.ats, ns, sz.slots), (sz.at2, n2, sz.own))
        ):
            for i in range(GROUP):
                tab[at + n + i] = dummy * 256
            tab[sz.head + 1 + k] = divide(n + GROUP - 1, GROUP)
        for i in range(5, 8):
            tab[sz.head + i] = 0

    return pl.pallas_call(
        kernel,
        out_shape=jax.ShapeDtypeStruct((sz.table,), jnp.int32),
        in_specs=[SMEM_SPEC] * (count + 2),
        out_specs=SMEM_SPEC,
        scratch_shapes=[pltpu.SMEM((sz.slots,), jnp.int32)],
    )(*pairs, send_all, where)


def select_row(ref, b):
    value = ref[...].astype(F32)
    rows = lax.broadcasted_iota(jnp.int32, value.shape, 0)
    return jnp.sum(jnp.where(rows == b, value, 0.0), axis=0, keepdims=True)


def outgoing_blocks(sz, send, where, positions, scales, start):
    def kernel(send_ref, where_ref, points, spreads, vectors, *outs):
        c = where_ref[0]
        for m in range(1, sz.peers):
            for q in range(sz.cap):
                b = send_ref[0, jnp.bitwise_xor(c, m) * sz.cap + q]
                b = jnp.minimum(b, sz.blocks - 1)
                out = outs[m - 1]
                out[q, 0 : sz.comps] = points[b]
                out[q, sz.comps : sz.comps + sz.vectors] = vectors[b]
                row = jnp.broadcast_to(select_row(spreads, b), (16, sz.width))
                out[q, sz.comps + sz.vectors :] = row.astype(BF16)

    shape = jax.ShapeDtypeStruct((sz.cap, sz.bundle, sz.width), BF16)
    return pl.pallas_call(
        kernel,
        out_shape=(shape,) * (sz.peers - 1),
        in_specs=[SMEM_SPEC] * 2 + [VMEM_SPEC] * 3,
        out_specs=(VMEM_SPEC,) * (sz.peers - 1),
        compiler_params=params(),
    )(send, where, positions, scales, start)


def split3(value):
    first = value.astype(BF16)
    rest = value - first.astype(F32)
    second = rest.astype(BF16)
    third = (rest - second.astype(F32)).astype(BF16)
    return first, second, third


def fill_factors(points, spread_row, left, right):
    comps = points.shape[0]
    x = points.astype(F32)
    inverse = 1.0 / spread_row
    norms = jnp.sum(x * x, axis=0, keepdims=True)
    y = x * (inverse * math.sqrt(2.0 * LOG2E))
    high = y.astype(BF16)
    low = (y - high.astype(F32)).astype(BF16)
    a1, a2, a3 = split3(norms * inverse * LOG2E)
    b1, b2, b3 = split3(inverse)
    left[0:comps] = high
    left[comps : 2 * comps] = low
    left[2 * comps : 3 * comps] = high
    right[0:comps] = high
    right[comps : 2 * comps] = high
    right[2 * comps : 3 * comps] = low
    shape = (16, points.shape[1])
    row = lax.broadcasted_iota(jnp.int32, shape, 0)
    lefts = (-a1, -a1, -a2, -a2, -a1, -a3, -b1, -b2, -b1, -b2, -b3, -b1)
    rights = (b1, b2, b1, b2, b3, b1, a1, a1, a2, a2, a1, a3)
    l_rest = jnp.zeros(shape, F32)
    r_rest = jnp.zeros(shape, F32)
    for k, (l_row, r_row) in enumerate(zip(lefts, rights)):
        l_rest = jnp.where(row == k, l_row.astype(F32), l_rest)
        r_rest = jnp.where(row == k, r_row.astype(F32), r_rest)
    at = 3 * comps
    left[at : at + 16] = l_rest.astype(BF16)
    right[at : at + 16] = r_rest.astype(BF16)
    unused = jnp.zeros((DEPTH - at - 16, points.shape[1]), BF16)
    left[at + 16 :] = unused
    right[at + 16 :] = unused


def segments(sz, tab, name):
    g0, g1, gs, g2 = (tab[sz.head + 1 + k] for k in range(4))
    if name == "0":
        return sz.at0, g0, 0
    if name == "1":
        return sz.at1, g1, g0
    if name == "S":
        return sz.ats, gs, g0 + g1
    return sz.at2, g2, g0 + g1 + gs


def entry(tab, place):
    code = tab[place]
    return lax.shift_right_arithmetic(code, jnp.int32(8)), jnp.bitwise_and(code, jnp.int32(255))


def row_block(sz, tab, name, row):
    if name == "S":
        return sz.blocks + jnp.minimum(row, sz.slots - 1)
    return tab[sz.head] * sz.own + jnp.minimum(row, sz.own - 1)


def partner_block(sz, name, partner):
    return sz.blocks + partner if name == "2" else partner


def build_tiles(sz, table, names, positions, scales, bundles, earlier):
    first = earlier is None
    many = len(bundles)
    held = sz.blocks + (sz.slots if many else 0)
    sum_rows = sz.own + 1 + sz.slots + 1
    writes = 3

    def kernel(*refs):
        tab, points, spreads = refs[:3]
        bundle_refs, refs = refs[3 : 3 + many], refs[3 + many :]
        if first:
            store, sum_out, left, right, ring, sem = refs
            sums = sum_out
            sums[...] = jnp.zeros(sums.shape, F32)
        else:
            _, old, store, sum_out, left, right, ring, sem, sums = refs
            sums[...] = old[...]

        def local(b, carry):
            fill_factors(points[b], select_row(spreads, b), left.at[b], right.at[b])
            return carry

        lax.fori_loop(0, sz.blocks, local, 0)
        for m in range(1, many + 1):

            def far(q, carry, m=m):
                at = sz.blocks + m * sz.cap + q
                bundle = bundle_refs[m - 1]
                row = bundle[q, sz.comps + sz.vectors :][0:1].astype(F32)
                fill_factors(bundle[q, 0 : sz.comps], row, left.at[at], right.at[at])
                return carry

            lax.fori_loop(0, sz.cap, far, 0)

        def write(slot, step):
            return pltpu.make_async_copy(
                ring.at[slot], store.at[pl.ds(step * GROUP, GROUP)], sem.at[slot]
            )

        done = jnp.int32(0)
        for name in names:
            table_at, steps, place = segments(sz, tab, name)
            base = 0 if name != "S" else sz.own + 1

            def step(t, carry, name=name, table_at=table_at, place=place, base=base, done=done):
                slot = lax.rem(done + t, writes)

                @pl.when(done + t >= writes)
                def _():
                    write(slot, 0).wait()

                for k in range(GROUP):
                    row, partner = entry(tab, table_at + t * GROUP + k)
                    r = row_block(sz, tab, name, row)
                    p = partner_block(sz, name, partner)
                    kernel_tile = jnp.exp2(dot(left[p], right[r], 0, 0))
                    ring[slot, k] = kernel_tile.astype(BF16)
                    sums[base + row] += jnp.sum(
                        kernel_tile.reshape(sz.width // 8, 8, sz.width), axis=0
                    )
                write(slot, jnp.minimum(place + t, STORED // GROUP)).start()
                return carry

            lax.fori_loop(0, steps, step, 0)
            done = done + steps
        for slot in range(writes):

            @pl.when(done >= slot + 1)
            def _(slot=slot):
                write(slot, 0).wait()

        if not first:
            for row in range(sz.own):
                sum_out[row : row + 1] = jnp.sum(sums[row], axis=0, keepdims=True)
            for row in range(sz.slots):
                at = sz.own + row
                sum_out[at : at + 1] = jnp.sum(sums[at + 1], axis=0, keepdims=True)

    tile_shape = jax.ShapeDtypeStruct((STORED + GROUP, sz.width, sz.width), BF16)
    sums_shape = (sum_rows, 8, sz.width)
    args = [table, positions, scales, *bundles]
    specs = [SMEM_SPEC] + [VMEM_SPEC] * (2 + many)
    scratch = [
        pltpu.VMEM((held, DEPTH, sz.width), BF16),
        pltpu.VMEM((held, DEPTH, sz.width), BF16),
        pltpu.VMEM((writes, GROUP, sz.width, sz.width), BF16),
        pltpu.SemaphoreType.DMA((writes,)),
    ]
    aliases = {}
    if not first:
        aliases = {len(args): 0}
        args += list(earlier)
        specs += [ANY_SPEC, VMEM_SPEC]
        scratch.append(pltpu.VMEM(sums_shape, F32))
        sums_shape = (sz.own + sz.slots, sz.width)
    entries = 64 if first else 28
    return pl.pallas_call(
        kernel,
        out_shape=(tile_shape, jax.ShapeDtypeStruct(sums_shape, F32)),
        in_specs=specs,
        out_specs=(ANY_SPEC, VMEM_SPEC),
        scratch_shapes=scratch,
        input_output_aliases=aliases,
        compiler_params=params(),
        cost_estimate=pl.CostEstimate(
            flops=2 * entries * sz.width**2 * DEPTH,
            bytes_accessed=2 * entries * sz.width**2,
            transcendentals=entries * sz.width**2,
        ),
    )(*args)


def group_sums(sz, table, around):
    def kernel(tab, *refs):
        parts, out = refs[: sz.cols], refs[sz.cols]
        z = tab[sz.head]
        for s in range(sz.cols):
            owner = lax.rem(z - s + sz.cols, sz.cols)
            for b in range(sz.own):
                out[pl.ds(owner * sz.own + b, 1), :] = parts[s][b : b + 1]
        slots = parts[0][sz.own :]
        for s in range(1, sz.cols):
            slots += parts[s][sz.own :]
        out[sz.blocks :] = slots

    return pl.pallas_call(
        kernel,
        out_shape=jax.ShapeDtypeStruct((sz.blocks + sz.slots, sz.width), F32),
        in_specs=[SMEM_SPEC] + [VMEM_SPEC] * sz.cols,
        out_specs=VMEM_SPEC,
    )(table, *around)


def scale_start(sz, table, send_all, where, partial, start, bundles):
    def kernel(tab, send_ref, where_ref, *refs):
        parts = refs[: sz.peers]
        start_ref = refs[sz.peers]
        far_refs = refs[sz.peers + 1 : 2 * sz.peers]
        near_out, far_out, root_out, total = refs[2 * sz.peers :]
        c = where_ref[0]
        for m in range(sz.peers):
            total[m, 0 : sz.blocks] = parts[m][0 : sz.blocks]
        for m in range(sz.peers):
            for k in range(sz.peers):
                if k == m:
                    continue
                for q in range(sz.cap):
                    b = send_ref[m, jnp.bitwise_xor(c, k) * sz.cap + q]
                    at = sz.blocks + (k ^ m) * sz.cap + q
                    total[m, pl.ds(b, 1), :] += parts[k][at : at + 1, :]
        root = lax.rsqrt(total[0, 0 : sz.blocks])
        root_out[...] = root
        for b in range(sz.blocks):
            near_out[b] = (root[b : b + 1] * start_ref[b].astype(F32)).astype(BF16)
        far_out[0 : sz.cap] = jnp.zeros((sz.cap, sz.vectors, sz.width), BF16)
        for m in range(1, sz.peers):
            for q in range(sz.cap):
                b = jnp.minimum(tab[sz.theirs + m * sz.cap + q], sz.blocks - 1)
                far_root = lax.rsqrt(total[m, pl.ds(b, 1), :])
                far_out[m * sz.cap + q] = (far_root * far_refs[m - 1][q, sz.comps : sz.comps + sz.vectors].astype(F32)).astype(BF16)

    return pl.pallas_call(
        kernel,
        out_shape=(
            jax.ShapeDtypeStruct((sz.blocks, sz.vectors, sz.width), BF16),
            jax.ShapeDtypeStruct((sz.slots, sz.vectors, sz.width), BF16),
            jax.ShapeDtypeStruct((sz.blocks, sz.width), F32),
        ),
        in_specs=[SMEM_SPEC] * 3 + [VMEM_SPEC] * (2 * sz.peers),
        out_specs=(VMEM_SPEC,) * 3,
        scratch_shapes=[pltpu.VMEM((sz.peers, sz.blocks + 8, sz.width), F32)],
        compiler_params=params(),
    )(table, send_all, where, *partial, start, *bundles)


def sweep_scratch(sz, held):
    return [
        pltpu.VMEM((held, sz.vectors, sz.width), BF16),
        pltpu.VMEM((RING, GROUP, sz.width, sz.width), BF16),
        pltpu.SemaphoreType.DMA((RING,)),
        pltpu.SemaphoreType.DMA((max(sz.cols, sz.peers),)),
        pltpu.VMEM((sz.bundle, sz.width), BF16),
        pltpu.VMEM((2, DEPTH, sz.width), BF16),
        pltpu.SemaphoreType.DMA((1,)),
    ]


class Stream:
    def __init__(self, sz, tab, names, store, geometry, scratch):
        self.sz, self.tab, self.name, self.store, self.geometry = sz, tab, names[-1], store, geometry
        _, self.ring, self.sem, _, self.x, self.factors, self.xsem = scratch
        self.table_at, self.steps, self.place = segments(sz, tab, names[0])
        self.split = None
        if len(names) > 1:
            self.split = self.steps
            self.second_at, steps, _ = segments(sz, tab, names[1])
            self.steps = self.steps + steps

    def entries(self, t):
        if self.split is None:
            return self.table_at + t * GROUP
        after = self.second_at + (t - self.split) * GROUP
        return jnp.where(t < self.split, self.table_at + t * GROUP, after)

    def read(self, t):
        slot = lax.rem(t, RING)
        return pltpu.make_async_copy(
            self.store.at[pl.ds((self.place + t) * GROUP, GROUP)], self.ring.at[slot], self.sem.at[slot]
        )

    def stored(self, t):
        return jnp.logical_and(t < self.steps, self.place + t < STORED // GROUP)

    def begin(self):
        for t in range(RING - 1):

            @pl.when(self.stored(t))
            def _(t=t):
                self.read(t).start()

    def factors_of(self, place):
        sz = self.sz
        points, scales, bundles = self.geometry

        def fetch(source, rows):
            copy = pltpu.make_async_copy(source, self.x.at[pl.ds(0, rows)], self.xsem.at[0])
            copy.start()
            copy.wait()

        @pl.when(place < sz.blocks)
        def _():
            fetch(points.at[place], sz.comps)

        slot = place - sz.blocks
        for m in range(1, sz.peers):

            @pl.when(jnp.logical_and(slot >= m * sz.cap, slot < (m + 1) * sz.cap))
            def _(m=m):
                fetch(bundles[m - 1].at[slot - m * sz.cap], sz.bundle)

        far_row = self.x[sz.comps + sz.vectors :][0:1].astype(F32)
        row = jnp.where(place < sz.blocks, select_row(scales, place), far_row)
        fill_factors(self.x[0 : sz.comps], row, self.factors.at[0], self.factors.at[1])

    def rebuild(self, t):
        slot = lax.rem(t, RING)

        def one(k, carry):
            row, partner = entry(self.tab, self.entries(t) + k)
            self.factors_of(partner_block(self.sz, self.name, partner))
            left = self.factors[0]
            self.factors_of(row_block(self.sz, self.tab, self.name, row))
            self.ring[slot, k] = jnp.exp2(dot(left, self.factors[1], 0, 0)).astype(BF16)
            return carry

        lax.fori_loop(0, GROUP, one, 0)

    def run(self, vectors, target):
        def step(t, carry):
            ahead = t + RING - 1

            @pl.when(self.stored(ahead))
            def _():
                self.read(ahead).start()

            have = self.stored(t)

            @pl.when(have)
            def _():
                self.read(t).wait()

            @pl.when(jnp.logical_not(have))
            def _():
                self.rebuild(t)

            slot = lax.rem(t, RING)
            for k in range(GROUP):
                row, partner = entry(self.tab, self.entries(t) + k)
                target[row] += dot(vectors[partner], self.ring[slot, k], 1, 0)
            return carry

        lax.fori_loop(0, self.steps, step, 0)


def load_vectors(sz, tab, pieces, vbuf, sem):
    copies = []
    for s, piece in enumerate(pieces):
        if piece.shape[0] == sz.blocks and sz.cols > 1:
            target = vbuf
        else:
            owner = lax.rem(tab[sz.head] - s + sz.cols, sz.cols)
            target = vbuf.at[pl.ds(owner * sz.own, sz.own)]
        copies.append(pltpu.make_async_copy(piece, target, sem.at[s]))
    for copy in copies:
        copy.start()
    return copies


def sweep_cost(sz, entries):
    return pl.CostEstimate(
        flops=2 * entries * sz.width**2 * sz.vectors * 4,
        bytes_accessed=2 * entries * sz.width**2,
        transcendentals=0,
    )


def geometry_specs(sz):
    return [ANY_SPEC, VMEM_SPEC] + [ANY_SPEC] * (sz.peers - 1)


def split_geometry(sz, refs):
    return (refs[0], refs[1], refs[2 : sz.peers + 1]), refs[sz.peers + 1 :]


def slot_products(sz, table, tiles, geometry, pieces, inverse):
    count = len(pieces)
    others = sz.peers - 1
    with_picks = inverse is not None

    def kernel(tab, store, *refs):
        blocks, refs = split_geometry(sz, refs)
        if with_picks:
            inverse_ref, refs = refs[0], refs[1:]
        piece_refs, refs = refs[:count], refs[count:]
        outs, refs = refs[:others], refs[others:]
        if with_picks:
            picks, refs = refs[:others], refs[others:]
        total, refs = refs[0], refs[1:]
        stream = Stream(sz, tab, "S", store, blocks, refs)
        vbuf = refs[0]
        copies = load_vectors(sz, tab, piece_refs, vbuf, refs[3])
        stream.begin()
        total[...] = jnp.zeros(total.shape, F32)
        for copy in copies:
            copy.wait()
        if with_picks:
            for m in range(1, sz.peers):
                for q in range(sz.cap):
                    b = jnp.minimum(tab[sz.mine + m * sz.cap + q], sz.blocks - 1)
                    picks[m - 1][q] = vbuf[b]
        stream.run(vbuf, total)
        for m in range(1, sz.peers):
            for q in range(sz.cap):
                products = total[m * sz.cap + q]
                if with_picks:
                    products = dot(inverse_ref[...], products, 1, 0, lax.Precision.HIGHEST)
                outs[m - 1][q] = products.astype(BF16)

    dims = (sz.cap, sz.vectors, sz.width)
    shapes = (jax.ShapeDtypeStruct(dims, BF16),) * others
    args = [table, tiles, *geometry]
    specs = [SMEM_SPEC, ANY_SPEC] + geometry_specs(sz)
    if with_picks:
        shapes *= 2
        args.append(inverse)
        specs.append(VMEM_SPEC)
    return pl.pallas_call(
        kernel,
        out_shape=shapes,
        in_specs=specs + [ANY_SPEC] * count,
        out_specs=(VMEM_SPEC,) * len(shapes),
        scratch_shapes=[pltpu.VMEM((sz.slots + 1, sz.vectors, sz.width), F32)]
        + sweep_scratch(sz, sz.blocks),
        compiler_params=params(),
        cost_estimate=sweep_cost(sz, 12),
    )(*args, *pieces)


def local_products(sz, table, tiles, geometry, pieces, names, earlier):
    count = len(pieces)
    first = earlier is None

    def kernel(tab, store, *refs):
        blocks, refs = split_geometry(sz, refs)
        piece_refs, refs = refs[:count], refs[count:]
        if not first:
            summed, refs = refs[0], refs[1:]
        out, total, refs = refs[0], refs[1], refs[2:]
        stream = Stream(sz, tab, names, store, blocks, refs)
        vbuf = refs[0]
        copies = load_vectors(sz, tab, piece_refs, vbuf, refs[3])
        stream.begin()
        if first:
            total[...] = jnp.zeros(total.shape, F32)
        else:
            total[0 : sz.own] = summed[...]
        for copy in copies:
            copy.wait()
        stream.run(vbuf, total)
        out[...] = total[0 : sz.own]

    args = [table, tiles, *geometry, *pieces]
    specs = [SMEM_SPEC, ANY_SPEC] + geometry_specs(sz) + [ANY_SPEC] * count
    if not first:
        args.append(earlier)
        specs.append(VMEM_SPEC)
    return pl.pallas_call(
        kernel,
        out_shape=jax.ShapeDtypeStruct((sz.own, sz.vectors, sz.width), F32),
        in_specs=specs,
        out_specs=VMEM_SPEC,
        scratch_shapes=[pltpu.VMEM((sz.own + 1, sz.vectors, sz.width), F32)]
        + sweep_scratch(sz, sz.blocks),
        compiler_params=params(),
        cost_estimate=sweep_cost(sz, sum(dict(zip("01", (18, 44)))[name] for name in names)),
    )(*args)


def far_products(sz, table, tiles, geometry, summed, far, returned, root, inverse):
    cells_total = sz.blocks * sz.width * sz.peers
    last = inverse is not None
    many = len(far)

    def kernel(tab, store, *refs):
        blocks, refs = split_geometry(sz, refs)
        summed_ref, root_ref, refs = refs[0], refs[1], refs[2:]
        if last:
            inverse_ref, refs = refs[0], refs[1:]
        far_refs, refs = refs[:many], refs[many:]
        back_refs, refs = refs[: sz.peers - 1], refs[sz.peers - 1 :]
        out, gram_out, total, refs = refs[0], refs[1], refs[2], refs[3:]
        stream = Stream(sz, tab, "2", store, blocks, refs[:7])
        vbuf, sem = refs[0], refs[3]
        if many == 1:
            copies = [pltpu.make_async_copy(far_refs[0], vbuf, sem.at[0])]
        else:
            copies = [
                pltpu.make_async_copy(far_refs[m - 1], vbuf.at[pl.ds(m * sz.cap, sz.cap)], sem.at[m])
                for m in range(1, sz.peers)
            ]
        for copy in copies:
            copy.start()
        stream.begin()
        z = tab[sz.head]
        total[0 : sz.own] = summed_ref[...]
        back = refs[-1] if last else total
        if last:
            back[...] = jnp.zeros(back.shape, F32)
        for m in range(1, sz.peers):
            for q in range(sz.cap):
                b = tab[sz.mine + m * sz.cap + q]

                @pl.when(divide(b, sz.own) == z)
                def _(m=m, q=q, b=b):
                    back[b - z * sz.own] += back_refs[m - 1][q].astype(F32)

        for copy in copies:
            copy.wait()
        stream.run(vbuf, total)
        gram = jnp.zeros((sz.vectors, sz.vectors), F32)
        for b in range(sz.own):
            root_row = root_ref[pl.ds(z * sz.own + b, 1), :]
            mapped = root_row * total[b]
            if last:
                mapped = dot(inverse_ref[...], mapped, 1, 0, lax.Precision.HIGHEST)
                mapped += root_row * back[b]
                out[b] = mapped
            else:
                out[b] = (root_row * mapped).astype(BF16)
            gram += dot(mapped, mapped, 1, 1, lax.Precision.HIGHEST)
        gram_out[...] = gram / cells_total

    args = [table, tiles, *geometry, summed, root]
    specs = [SMEM_SPEC, ANY_SPEC] + geometry_specs(sz) + [VMEM_SPEC] * 2
    if last:
        args.append(inverse)
        specs.append(VMEM_SPEC)
    args += [*far, *returned]
    specs += [ANY_SPEC] * many + [VMEM_SPEC] * len(returned)
    return pl.pallas_call(
        kernel,
        out_shape=(
            jax.ShapeDtypeStruct((sz.own, sz.vectors, sz.width), F32 if last else BF16),
            jax.ShapeDtypeStruct((sz.vectors, sz.vectors), F32),
        ),
        in_specs=specs,
        out_specs=(VMEM_SPEC, VMEM_SPEC),
        scratch_shapes=[pltpu.VMEM((sz.own + 1, sz.vectors, sz.width), F32)]
        + sweep_scratch(sz, sz.slots)
        + [pltpu.VMEM((sz.own, sz.vectors, sz.width), F32)] * last,
        compiler_params=params(),
        cost_estimate=sweep_cost(sz, 20),
    )(*args)


def inverse_factor(gram):
    n = gram.shape[0]
    eye = (
        lax.broadcasted_iota(jnp.int32, (n, n), 0) == lax.broadcasted_iota(jnp.int32, (n, n), 1)
    ).astype(F32)
    whole = jnp.concatenate([gram, eye], axis=1)
    chunk = 8
    parts = [whole[i : i + chunk] for i in range(0, n, chunk)]
    row_ids = lax.broadcasted_iota(jnp.int32, (chunk, 1), 0)
    for k in range(n):
        at, inside = k // chunk, k % chunk
        row = parts[at][inside : inside + 1]
        pivot = row[:, k : k + 1]
        ratio = row / pivot
        for j in range(at, n // chunk):
            factor = parts[j][:, k : k + 1]
            if j == at:
                if inside == chunk - 1:
                    continue
                factor = jnp.where(row_ids > inside, factor, 0.0)
            parts[j] = parts[j] - factor * ratio
    out = []
    for j in range(n // chunk):
        diagonal = jnp.sum(
            parts[j][:, :n] * eye[j * chunk : (j + 1) * chunk], axis=1, keepdims=True
        )
        out.append(parts[j][:, n:] * lax.rsqrt(diagonal))
    return jnp.concatenate(out, axis=0)


def factor_call(sz, gram):
    def kernel(gram_ref, out):
        out[...] = inverse_factor(gram_ref[...])

    return pl.pallas_call(
        kernel,
        out_shape=jax.ShapeDtypeStruct((sz.vectors, sz.vectors), F32),
        in_specs=[VMEM_SPEC],
        out_specs=VMEM_SPEC,
    )(gram)


def normalize(sz, table, gram, mapped):
    share = sz.vectors // sz.cols

    def kernel(tab, gram_ref, mapped_ref, *refs):
        outs, buf = refs[: sz.cols], refs[sz.cols]
        inverse = inverse_factor(gram_ref[...])
        z = tab[sz.head]
        for b in range(sz.own):
            buf[...] = dot(inverse, mapped_ref[b], 1, 0, lax.Precision.HIGHEST)
            for s in range(sz.cols):
                to = lax.rem(z + s, sz.cols)
                outs[s][b] = buf[pl.ds(pl.multiple_of(to * share, share), share)].astype(BF16)

    return pl.pallas_call(
        kernel,
        out_shape=(jax.ShapeDtypeStruct((sz.own, share, sz.width), BF16),) * sz.cols,
        in_specs=[SMEM_SPEC, VMEM_SPEC, VMEM_SPEC],
        out_specs=(VMEM_SPEC,) * sz.cols,
        scratch_shapes=[pltpu.VMEM((sz.vectors, sz.width), F32)],
        compiler_params=params(),
    )(table, gram, mapped)


def assemble(sz, table, pieces):
    share = sz.vectors // sz.cols

    def kernel(tab, *refs):
        out = refs[-1]
        z = tab[sz.head]
        for s in range(sz.cols):
            owner = lax.rem(z - s + sz.cols, sz.cols)
            for b in range(sz.own):
                out[owner * sz.own + b] = refs[s][b].astype(F32)

    return pl.pallas_call(
        kernel,
        out_shape=jax.ShapeDtypeStruct((sz.blocks, share, sz.width), F32),
        in_specs=[SMEM_SPEC] + [VMEM_SPEC] * sz.cols,
        out_specs=VMEM_SPEC,
        compiler_params=params(),
    )(table, *pieces)


def body(positions, scales, start_vectors, send_list, pair_rows, pair_partner):
    sz = Sizes(positions, start_vectors, send_list, pair_rows)
    where = jnp.stack([lax.axis_index("cells"), lax.axis_index("cols")]).astype(jnp.int32)
    n = sz.cols

    pairs = spread(
        jnp.concatenate([pair_rows.reshape(1, -1), pair_partner.reshape(1, -1)], axis=0), "cols"
    )
    lists = send_list.reshape(1, -1)
    send_all = jnp.concatenate([lists] + exchange([lists] * sz.peers, "cells"), axis=0)
    outgoing = outgoing_blocks(sz, lists, where, positions, scales, start_vectors)
    bundles = exchange((None,) + tuple(outgoing), "cells")

    table = build_table(sz, pairs, send_all, where)
    built = build_tiles(sz, table, "01", positions, scales, [], None)
    tiles, sums = build_tiles(sz, table, "S2", positions, scales, bundles, built)
    geometry = (positions, scales, *bundles)

    partial = group_sums(sz, table, spread(sums, "cols"))
    partials = [partial] + exchange([partial] * sz.peers, "cells")
    near, far, root = scale_start(sz, table, send_all, where, partials, start_vectors, bundles)

    sent = slot_products(sz, table, tiles, geometry, [near], None)
    returned = exchange((None,) + tuple(sent), "cells")
    summed = local_products(sz, table, tiles, geometry, [near], "01", None)
    scaled, gram = far_products(
        sz, table, tiles, geometry, summed, [far], returned, root, None
    )

    pieces = spread(scaled, "cols")
    gram = butterfly(sum(spread(gram, "cols")), "cells")
    summed = local_products(sz, table, tiles, geometry, [scaled], "0", None)
    first_inverse = factor_call(sz, gram)
    pieces, summed, first_inverse = lax.optimization_barrier((pieces, summed, first_inverse))
    sent = slot_products(sz, table, tiles, geometry, pieces, first_inverse)
    sent, picks = sent[: sz.peers - 1], sent[sz.peers - 1 :]
    far_pieces = exchange((None,) + tuple(picks), "cells")
    returned = exchange((None,) + tuple(sent), "cells")
    summed = local_products(sz, table, tiles, geometry, pieces, "1", summed)
    mapped, gram = far_products(
        sz, table, tiles, geometry, summed, far_pieces, returned, root, first_inverse
    )
    gram = butterfly(butterfly(gram, "cells"), "cols")
    shares = normalize(sz, table, gram, mapped)
    arrived = [shares[0]] + [
        lax.ppermute(shares[s], "cols", [(i, (i + s) % n) for i in range(n)]) for s in range(1, n)
    ]
    return assemble(sz, table, arrived)


def solution(mesh):
    in_specs = (
        P(("lineage", "cells"), None, None),
        P(("lineage", "cells"), None),
        P(("lineage", "cells"), None, None),
        P(("lineage", "cells"), None, None),
        P(("lineage", "cells"), "cols", None),
        P(("lineage", "cells"), "cols", None),
    )
    out_specs = P(("lineage", "cells"), "cols", None)
    return jax.shard_map(body, mesh=mesh, in_specs=in_specs, out_specs=out_specs, check_vma=False)
```

time: 246 us -> 209 us (0.85); the launches traced: 244 us -> 210 us
  local copies, waits for them, and re-layouts: 23 us -> 8.24 us
  waiting for transfers between devices: 43.8 us -> 30.6 us
  Pallas kernels: 126 us -> 119 us
  starting transfers between devices: 42.7 us -> 46 us
    ppermute x8 -> x6, waiting for transfers between devices: 31.6 us -> 12.3 us  [butterfly(): value = value + lax.ppermute(value, axis, [(i, i ^ step) for i in range(n)])]
    pallas_call x5 -> x7, Pallas kernels: 63.2 us -> 53.4 us  [the longest x2 30 us: build_tiles(): pl.pallas_call(kernel, out_shape=(tile_shape, jax.ShapeDtypeStruct(sums_s...]
    ppermute x8 -> x6, starting transfers between devices: 4.59 us -> 11.5 us  [butterfly(): value = value + lax.ppermute(value, axis, [(i, i ^ step) for i in range(n)])]
    ppermute x9 -> x12, waiting for transfers between devices: 4.82 us -> 10.7 us  [spread(): lax.ppermute(value, axis, [(i, (i + s) % n) for i in range(n)])]
    squeeze x5 -> x0, local copies, waits for them, and re-layouts: 5.64 us -> none  [the longest x3 3.3 us: exchange(): pieces[m]]
    pallas_call x2 -> x3, Pallas kernels: 28.6 us -> 34 us  [local_products(): pl.pallas_call(kernel, out_shape=jax.ShapeDtypeStruct((sz.own, sz.vectors...]
    gather x6 -> x0, local copies, waits for them, and re-layouts: 5.33 us -> none  [the longest x3 4.17 us: pick(): picked = jnp.take(values, listed, axis=0, mode='clip')]
    ppermute x24 -> x18, starting transfers between devices: 18.8 us -> 14.6 us  [exchange(): lax.ppermute(pieces[m], axis, [(i, i ^ m) for i in range(n)])]
  transfers between devices with their start and end apart: 44 -> 39, of which waited for: 17 -> 15; matrix products, arithmetic and copies ran while one was open for 7% -> 2% of each run, Pallas kernels for 33% -> 32%
where the time goes in v2:
time: 209 us; the launch traced here: 210 us
  Pallas kernels  119 us (57%)
  starting transfers between devices  46 us (22%)
  waiting for transfers between devices  30.6 us (15%)
  local copies, waits for them, and re-layouts  8.24 us (4%)
  other arithmetic  5.32 us (3%)
    pallas_call x3, Pallas kernels, local_products(): pl.pallas_call(kernel, out_shape=jax.ShapeDtypeStruct((sz.own, sz.vectors...  34 us
    pallas_call x2, Pallas kernels, build_tiles(): pl.pallas_call(kernel, out_shape=(tile_shape, jax.ShapeDtypeStruct(sums_s...  30 us
    ppermute x12, starting transfers between devices, spread(): lax.ppermute(value, axis, [(i, (i + s) % n) for i in range(n)])  15.6 us
    ppermute x18, starting transfers between devices, exchange(): lax.ppermute(pieces[m], axis, [(i, i ^ m) for i in range(n)])  14.6 us
    pallas_call x2, Pallas kernels, far_products(): pl.pallas_call(kernel, out_shape=(jax.ShapeDtypeStruct((sz.own, sz.vector...  14.5 us
    ppermute x6, waiting for transfers between devices, butterfly(): value = value + lax.ppermute(value, axis, [(i, i ^ step) for i in range(n)])  12.3 us
    pallas_call x2, Pallas kernels, slot_products(): pl.pallas_call(kernel, out_shape=shapes, in_specs=specs + [ANY_SPEC] * co...  11.6 us
    ppermute x6, starting transfers between devices, butterfly(): value = value + lax.ppermute(value, axis, [(i, i ^ step) for i in range(n)])  11.5 us
  transfers between devices with their start and end apart: 39, of which 15 were waited for; matrix products, arithmetic and copies ran while one was open for 2% of the time, Pallas kernels for 32%

profile of v2, /device:TPU:0, one launch (start us, length us, event | category | flops | bytes accessed | tf_op | source)
XLA Modules:
  0.0 209.6 jit_solution(7101708462715193359)
XLA Ops:
  0.0 0.8 copy.9
  0.9 2.4 %collective-permute-start.5 = (s32[1,8]{1,0:T(1,128)S(1)}, s32[1,8]{1,0:T(1,128)S(1)}, u32[]{:S(2)}, u32[]{:S(2)}) collective-permute-start(s32[1,8]{1,0:T(1,128)S(1)} %reshape.11.send_ref), channel_id=1, source_target_pairs={{0,12},{4,8},{8,4},{12,0},{1,13},{5,9},{9,5},{13,1},{2,14},{6,10},... | collective-permute-start | bytes 104 | tf_op jit(solution)/shard_map/ppermute | solution.py:37
  3.3 0.6 collective-permute-start.4
  3.9 0.7 pad_add_fusion.1.refs_0_
  4.6 3.9 %collective-permute-start.2 = (s32[2,48]{1,0:T(2,128)S(1)}, s32[2,48]{1,0:T(2,128)S(1)}, u32[]{:S(2)}, u32[]{:S(2)}) collective-permute-start(s32[2,48]{1,0:T(2,128)S(1)} %pad_add_fusion.1.refs_0_), channel_id=1, source_target_pairs={{0,3},{1,0},{2,1},{3,2},{4,7},{5,4},{6,5},{7,6},{8,11},{9,8},{10,9... | collective-permute-start | bytes 1160 | tf_op jit(solution)/shard_map/ppermute | solution.py:44
  8.5 0.7 pad_add_fusion.2.refs_5_.where_ref
  9.2 2.5 %shard_map.65 = (bf16[2,144,512]{2,1,0:T(8,128)(2,1)}, bf16[2,144,512]{2,1,0:T(8,128)(2,1)}, bf16[2,144,512]{2,1,0:T(8,128)(2,1)}) custom-call(s32[1,8]{1,0:T(1,128)} %copy-done.24, s32[2]{0:T(128)} %pad_add_fusion.2.refs_5_.where_ref, bf16[16,64,512]{2,1,0:T(8,128)(2,1)} %refs_0_.13, bf16[16,512]{1,0:T(8,128)(2,1)} %refs_1_.17, bf16[16,64,512]{2,1,0:T(8,128)(2,1)} %refs_4_.1), custom_call_target="tpu_custom_call" | custom-call | tf_op jit(solution)/shard_map/pallas_call | solution.py:181
  11.7 1.0 collective-permute-start
  12.7 1.6 collective-permute-start.7
  14.3 1.2 pad_add_fusion.refs_4_.send_ref
  15.8 1.3 collective-permute-done.refs_1_
  17.6 5.6 %shard_map.64.refs_0_.tab = s32[1192]{0:T(1024)} custom-call(s32[2,48]{1,0:T(2,128)} %copy-done.25, s32[2,48]{1,0:T(2,128)} %copy-done.28, s32[2,48]{1,0:T(2,128)} %copy-done.27, s32[2,48]{1,0:T(2,128)} %copy-done.26, s32[4,8]{1,0:T(4,128)} %pad_add_fusion.refs_4_.send_ref, s32[2]{0:T(128)} %pad_add_fusion.2.refs_5_.where_ref), custom_call_target="tpu_custom_call" | custom-call | tf_op jit(solution)/shard_map/pallas_call | solution.py:152
  23.2 19.1 %shard_map.66 = (bf16[164,512,512]{2,1,0:T(8,128)(2,1)}, f32[14,8,512]{2,1,0:T(8,128)}) custom-call(s32[1192]{0:T(1024)} %shard_map.64.refs_0_.tab, bf16[16,64,512]{2,1,0:T(8,128)(2,1)} %refs_0_.13, bf16[16,512]{1,0:T(8,128)(2,1)} %refs_1_.17), custom_call_target="tpu_custom_call" | custom-call | flops 8589934592 | bytes 33554432 | tf_op jit(solution)/shard_map/pallas_call | solution.py:353
  42.3 0.7 copy-done
  43.2 10.9 %shard_map.67 = (bf16[164,512,512]{2,1,0:T(8,128)(2,1)}, f32[12,512]{1,0:T(8,128)}) custom-call(s32[1192]{0:T(1024)} %shard_map.64.refs_0_.tab, bf16[16,64,512]{2,1,0:T(8,128)(2,1)} %refs_0_.13, bf16[16,512]{1,0:T(8,128)(2,1)} %refs_1_.17, bf16[2,144,512]{2,1,0:T(8,128)(2,1)} %copy-done, ...), custom_call_target="tpu_custom_call", output_to_operand_aliasing={{0}: (6, {})} | custom-call | flops 3758096384 | bytes 14680064 | tf_op jit(solution)/shard_map/pallas_call | solution.py:353
  54.1 3.0 %collective-permute-start.11 = (f32[12,512]{1,0:T(8,128)}, f32[12,512]{1,0:T(8,128)S(1)}, u32[]{:S(2)}, u32[]{:S(2)}) collective-permute-start(f32[12,512]{1,0:T(8,128)} %get-tuple-element.44.refs_0_), channel_id=1, source_target_pairs={{0,3},{1,0},{2,1},{3,2},{4,7},{5,4},{6,5},{7,6},{8,11},{9,8},{10,9... | collective-permute-start | bytes 73736 | tf_op jit(solution)/shard_map/ppermute | solution.py:44
  57.8 1.3 collective-permute-done.11.refs_3_
  59.1 3.1 %collective-permute-done.10.refs_2_ = f32[12,512]{1,0:T(8,128)S(1)} collective-permute-done((f32[12,512]{1,0:T(8,128)}, f32[12,512]{1,0:T(8,128)S(1)}, u32[]{:S(2)}, u32[]{:S(2)}) %collective-permute-start.10) | collective-permute-done | bytes 24608 | tf_op jit(solution)/shard_map/ppermute | solution.py:44
  62.2 1.1 collective-permute-done.9.refs_1_
  63.9 1.5 shard_map.68.refs_0_
  65.5 3.8 %collective-permute-start.14 = (f32[24,512]{1,0:T(8,128)}, f32[24,512]{1,0:T(8,128)S(1)}, u32[]{:S(2)}, u32[]{:S(2)}) collective-permute-start(f32[24,512]{1,0:T(8,128)} %shard_map.68.refs_0_), channel_id=1, source_target_pairs={{0,12},{4,8},{8,4},{12,0},{1,13},{5,9},{9,5},{13,1},{2,14},{6,10},... | collective-permute-start | bytes 147464 | tf_op jit(solution)/shard_map/ppermute | solution.py:37
  69.4 1.9 collective-permute-done.14.refs_3_
  71.3 2.2 %collective-permute-done.13.refs_2_ = f32[24,512]{1,0:T(8,128)S(1)} collective-permute-done((f32[24,512]{1,0:T(8,128)}, f32[24,512]{1,0:T(8,128)S(1)}, u32[]{:S(2)}, u32[]{:S(2)}) %collective-permute-start.13) | collective-permute-done | bytes 49184 | tf_op jit(solution)/shard_map/ppermute | solution.py:37
  73.6 0.6 copy-done.19
  74.2 0.6 copy-done.20
  74.8 2.9 %shard_map.69 = (bf16[16,64,512]{2,1,0:T(8,128)(2,1)}, bf16[8,64,512]{2,1,0:T(8,128)(2,1)}, f32[16,512]{1,0:T(8,128)}) custom-call(s32[1192]{0:T(1024)} %shard_map.64.refs_0_.tab, s32[4,8]{1,0:T(4,128)} %pad_add_fusion.refs_4_.send_ref, s32[2]{0:T(128)} %pad_add_fusion.2.refs_5_.where_ref, f32[24,512]{1,0:T(8,128)} %shard_map.68.refs_0_, ...), custom_call_target="tpu_custom_call" | custom-call | tf_op jit(solution)/shard_map/pallas_call | solution.py:418
  77.8 5.3 %shard_map.71 = (bf16[2,64,512]{2,1,0:T(8,128)(2,1)}, bf16[2,64,512]{2,1,0:T(8,128)(2,1)}, bf16[2,64,512]{2,1,0:T(8,128)(2,1)}) custom-call(s32[1192]{0:T(1024)} %shard_map.64.refs_0_.tab, bf16[164,512,512]{2,1,0:T(8,128)(2,1)} %get-tuple-element.43.store, bf16[16,64,512]{2,1,0:T(8,128)(2,1)} %refs_0_.13, bf16[16,512]{1,0:T(8,128)(2,1)} %refs_1_.17, ...), custom_call_target="tpu_custom_call" | custom-call | flops 1610612736 | bytes 6291456 | tf_op jit(solution)/shard_map/pallas_call | solution.py:613
  83.2 1.8 collective-permute-start.17
  85.0 14.5 %shard_map.70.refs_5_ = f32[4,64,512]{2,1,0:T(8,128)} custom-call(s32[1192]{0:T(1024)} %shard_map.64.refs_0_.tab, bf16[164,512,512]{2,1,0:T(8,128)(2,1)} %get-tuple-element.43.store, bf16[16,64,512]{2,1,0:T(8,128)(2,1)} %refs_0_.13, bf16[16,512]{1,0:T(8,128)(2,1)} %refs_1_.17, bf16[2,144,512]{2,1,0:T(8,128)(2,1)} %copy-done, bf16[2,144,512]{2,1,0:T(8,128)(2,1)} %copy-done.1, ...), custom_call_target="tpu_custom_call" | custom-call | flops 8321499136 | bytes 32505856 | tf_op jit(solution)/shard_map/pallas_call | solution.py:653
  100.2 6.8 %shard_map.72 = (bf16[4,64,512]{2,1,0:T(8,128)(2,1)}, f32[64,64]{1,0:T(8,128)}) custom-call(s32[1192]{0:T(1024)} %shard_map.64.refs_0_.tab, bf16[164,512,512]{2,1,0:T(8,128)(2,1)} %get-tuple-element.43.store, bf16[16,64,512]{2,1,0:T(8,128)(2,1)} %refs_0_.13, bf16[16,512]{1,0:T(8,128)(2,1)} %refs_1_.17, bf16[2,144,512]{2,1,0:T(8,128)(2,1)} %copy-done, ...), custom_call_target="tpu_custom_call" | custom-call | flops 2684354560 | bytes 10485760 | tf_op jit(solution)/shard_map/pallas_call | solution.py:726
  107.0 1.5 collective-permute-start.23
  108.5 0.6 collective-permute-start.21
  109.1 3.2 %collective-permute-start.20 = (bf16[4,64,512]{2,1,0:T(8,128)(2,1)}, bf16[4,64,512]{2,1,0:T(8,128)(2,1)S(1)}, u32[]{:S(2)}, u32[]{:S(2)}) collective-permute-start(bf16[4,64,512]{2,1,0:T(8,128)(2,1)} %get-tuple-element.53.refs_5_.refs_6_), channel_id=1, source_target_pairs={{0,3},{1,0},{2,1},{3,2},{4,7},{5,4},{6,5},{7,6},{8,11},{9,8},{10,9... | collective-permute-start | bytes 786440 | tf_op jit(solution)/shard_map/ppermute | solution.py:44
  112.3 1.1 collective-permute-start.19
  113.4 0.6 collective-permute-start.18
  114.0 0.7 collective-permute-done.21
  114.7 0.8 add_add_fusion
  115.6 1.2 collective-permute-done.24
  116.8 3.0 %collective-permute-start.25 = (f32[64,64]{1,0:T(8,128)S(1)}, f32[64,64]{1,0:T(8,128)S(1)}, u32[]{:S(2)}, u32[]{:S(2)}) collective-permute-start(f32[64,64]{1,0:T(8,128)S(1)} %add.30), channel_id=1, source_target_pairs={{0,8},{4,12},{8,0},{12,4},{1,9},{5,13},{9,1},{13,5},{2,10},{6,14},... | collective-permute-start | bytes 49160 | tf_op jit(solution)/shard_map/ppermute | solution.py:52
  119.8 6.7 %shard_map.73.refs_9_ = f32[4,64,512]{2,1,0:T(8,128)} custom-call(s32[1192]{0:T(1024)} %shard_map.64.refs_0_.tab, bf16[164,512,512]{2,1,0:T(8,128)(2,1)} %get-tuple-element.43.store, bf16[16,64,512]{2,1,0:T(8,128)(2,1)} %refs_0_.13, bf16[16,512]{1,0:T(8,128)(2,1)} %refs_1_.17, bf16[2,144,512]{2,1,0:T(8,128)(2,1)} %copy-done, bf16[2,144,512]{2,1,0:T(8,128)(2,1)} %copy-done.1, ...), custom_call_target="tpu_custom_call" | custom-call | flops 2415919104 | bytes 9437184 | tf_op jit(solution)/shard_map/pallas_call | solution.py:653
  127.2 6.8 %shard_map.74.refs_5_.refs_7_ = f32[64,64]{1,0:T(8,128)} custom-call(f32[64,64]{1,0:T(8,128)} %add.31.gram_ref), custom_call_target="tpu_custom_call" | custom-call | tf_op jit(solution)/shard_map/pallas_call | solution.py:776
  134.0 3.3 %collective-permute-done.19.refs_7_.refs_8_ = bf16[4,64,512]{2,1,0:T(8,128)(2,1)S(1)} collective-permute-done((bf16[4,64,512]{2,1,0:T(8,128)(2,1)}, bf16[4,64,512]{2,1,0:T(8,128)(2,1)S(1)}, u32[]{:S(2)}, u32[]{:S(2)}) %collective-permute-start.19) | collective-permute-done | bytes 262176 | tf_op jit(solution)/shard_map/ppermute | solution.py:44
  137.2 0.7 copy-done.4
  137.9 0.7 copy-done.5
  138.6 6.3 %shard_map.76 = (bf16[2,64,512]{2,1,0:T(8,128)(2,1)}, bf16[2,64,512]{2,1,0:T(8,128)(2,1)}, bf16[2,64,512]{2,1,0:T(8,128)(2,1)}, bf16[2,64,512]{2,1,0:T(8,128)(2,...) custom-call(s32[1192]{0:T(1024)} %shard_map.64.refs_0_.tab, ...), custom_call_target="tpu_custom_call" | custom-call | flops 1610612736 | bytes 6291456 | tf_op jit(solution)/shard_map/pallas_call | solution.py:613
  145.1 1.8 collective-permute-start.28
  147.4 1.4 collective-permute-start.31
  148.8 12.7 %shard_map.75.refs_5_ = f32[4,64,512]{2,1,0:T(8,128)} custom-call(s32[1192]{0:T(1024)} %shard_map.64.refs_0_.tab, bf16[164,512,512]{2,1,0:T(8,128)(2,1)} %get-tuple-element.43.store, bf16[16,64,512]{2,1,0:T(8,128)(2,1)} %refs_0_.13, bf16[16,512]{1,0:T(8,128)(2,1)} %refs_1_.17, bf16[2,144,512]{2,1,0:T(8,128)(2,1)} %copy-done, bf16[2,144,512]{2,1,0:T(8,128)(2,1)} %copy-done.1, ...), custom_call_target="tpu_custom_call" | custom-call | flops 5905580032 | bytes 23068672 | tf_op jit(solution)/shard_map/pallas_call | solution.py:653
  162.3 0.7 copy-done.11
  163.0 7.8 %shard_map.77 = (f32[4,64,512]{2,1,0:T(8,128)}, f32[64,64]{1,0:T(8,128)}) custom-call(s32[1192]{0:T(1024)} %shard_map.64.refs_0_.tab, bf16[164,512,512]{2,1,0:T(8,128)(2,1)} %get-tuple-element.43.store, bf16[16,64,512]{2,1,0:T(8,128)(2,1)} %refs_0_.13, bf16[16,512]{1,0:T(8,128)(2,1)} %refs_1_.17, bf16[2,144,512]{2,1,0:T(8,128)(2,1)} %copy-done, ...), custom_call_target="tpu_custom_call" | custom-call | flops 2684354560 | bytes 10485760 | tf_op jit(solution)/shard_map/pallas_call | solution.py:726
  170.9 1.4 collective-permute-done.32
  172.3 0.8 add.32
  173.4 3.5 %collective-permute-done.33 = f32[64,64]{1,0:T(8,128)S(1)} collective-permute-done((f32[64,64]{1,0:T(8,128)S(1)}, f32[64,64]{1,0:T(8,128)S(1)}, u32[]{:S(2)}, u32[]{:S(2)}) %collective-permute-start.33) | collective-permute-done | bytes 16416 | tf_op jit(solution)/shard_map/ppermute | solution.py:52
  176.9 7.4 %collective-permute-start.34 = (f32[64,64]{1,0:T(8,128)S(1)}, f32[64,64]{1,0:T(8,128)S(1)}, u32[]{:S(2)}, u32[]{:S(2)}) collective-permute-start(f32[64,64]{1,0:T(8,128)S(1)} %add.33), channel_id=1, source_target_pairs={{0,1},{1,0},{2,3},{3,2},{4,5},{5,4},{6,7},{7,6},{8,9},{9,8},{10,11... | collective-permute-start | bytes 49160 | tf_op jit(solution)/shard_map/ppermute | solution.py:52
  184.3 1.9 collective-permute-done.34
  186.7 4.4 %collective-permute-done.35 = f32[64,64]{1,0:T(8,128)S(1)} collective-permute-done((f32[64,64]{1,0:T(8,128)S(1)}, f32[64,64]{1,0:T(8,128)S(1)}, u32[]{:S(2)}, u32[]{:S(2)}) %collective-permute-start.35) | collective-permute-done | bytes 16416 | tf_op jit(solution)/shard_map/ppermute | solution.py:52
  191.1 0.6 add.35.gram_ref
  191.7 7.8 %shard_map.78 = (bf16[4,16,512]{2,1,0:T(8,128)(2,1)}, bf16[4,16,512]{2,1,0:T(8,128)(2,1)}, bf16[4,16,512]{2,1,0:T(8,128)(2,1)}, bf16[4,16,512]{2,1,0:T(8,128)(2,1)}) custom-call(s32[1192]{0:T(1024)} %shard_map.64.refs_0_.tab, f32[64,64]{1,0:T(8,128)} %add.35.gram_ref, f32[4,64,512]{2,1,0:T(8,128)} %get-tuple-element.66.mapped_ref), custom_call_target="tpu_custom_call" | custom-call | tf_op jit(solution)/shard_map/pallas_call | solution.py:797
  199.5 2.0 collective-permute-start.36
  201.7 2.1 %collective-permute-start.38 = (bf16[4,16,512]{2,1,0:T(8,128)(2,1)}, bf16[4,16,512]{2,1,0:T(8,128)(2,1)S(1)}, u32[]{:S(2)}, u32[]{:S(2)}) collective-permute-start(bf16[4,16,512]{2,1,0:T(8,128)(2,1)} %get-tuple-element.70), channel_id=1, source_target_pairs={{0,3},{1,0},{2,1},{3,2},{4,7},{5,4},{6,5},{7,6},{8,11},{9,8},{10,9... | collective-permute-start | bytes 196616 | tf_op jit(solution)/shard_map/ppermute | solution.py:872
  203.8 1.9 collective-permute-done.36.refs_1_
  205.7 1.4 collective-permute-done.37.refs_2_
  207.1 0.6 copy-done.16
  207.8 1.8 shard_map.79
  (100 shorter events, 6.7 us)
Async XLA Ops:
  0.9 8.3 %copy-start.24 = (s32[1,8]{1,0:T(1,128)}, s32[1,8]{1,0:T(1,128)S(1)}, u32[]{:S(2)}) copy-start(s32[1,8]{1,0:T(1,128)S(1)} %reshape.11.send_ref) | copy-start | bytes 100
  0.9 10.9 %collective-permute-start.5 = (s32[1,8]{1,0:T(1,128)S(1)}, s32[1,8]{1,0:T(1,128)S(1)}, u32[]{:S(2)}, u32[]{:S(2)}) collective-permute-start(s32[1,8]{1,0:T(1,128)S(1)} %reshape.11.send_ref), channel_id=1, source_target_pairs={{0,12},{4,8},{8,4},{12,0},{1,13},{5,9},{9,5},{13,1},{2,14},{6,10},... | collective-permute-start | bytes 104 | tf_op jit(solution)/shard_map/ppermute | solution.py:37
  3.3 9.5 %collective-permute-start.4 = (s32[1,8]{1,0:T(1,128)S(1)}, s32[1,8]{1,0:T(1,128)S(1)}, u32[]{:S(2)}, u32[]{:S(2)}) collective-permute-start(s32[1,8]{1,0:T(1,128)S(1)} %reshape.11.send_ref), channel_id=1, source_target_pairs={{0,8},{4,12},{8,0},{12,4},{1,9},{5,13},{9,1},{13,5},{2,10},{6,14},... | collective-permute-start | bytes 104 | tf_op jit(solution)/shard_map/ppermute | solution.py:37
  3.9 8.8 %collective-permute-start.3 = (s32[1,8]{1,0:T(1,128)S(1)}, s32[1,8]{1,0:T(1,128)S(1)}, u32[]{:S(2)}, u32[]{:S(2)}) collective-permute-start(s32[1,8]{1,0:T(1,128)S(1)} %reshape.11.send_ref), channel_id=1, source_target_pairs={{0,4},{4,0},{8,12},{12,8},{1,5},{5,1},{9,13},{13,9},{2,6},{6,2},{1... | collective-permute-start | bytes 104 | tf_op jit(solution)/shard_map/ppermute | solution.py:37
  4.6 12.5 %copy-start.25 = (s32[2,48]{1,0:T(2,128)}, s32[2,48]{1,0:T(2,128)S(1)}, u32[]{:S(2)}) copy-start(s32[2,48]{1,0:T(2,128)S(1)} %pad_add_fusion.1.refs_0_) | copy-start | bytes 1156
  4.6 10.9 %collective-permute-start.2 = (s32[2,48]{1,0:T(2,128)S(1)}, s32[2,48]{1,0:T(2,128)S(1)}, u32[]{:S(2)}, u32[]{:S(2)}) collective-permute-start(s32[2,48]{1,0:T(2,128)S(1)} %pad_add_fusion.1.refs_0_), channel_id=1, source_target_pairs={{0,3},{1,0},{2,1},{3,2},{4,7},{5,4},{6,5},{7,6},{8,11},{9,8},{10,9... | collective-permute-start | bytes 1160 | tf_op jit(solution)/shard_map/ppermute | solution.py:44
  8.5 7.3 %collective-permute-start.1 = (s32[2,48]{1,0:T(2,128)S(1)}, s32[2,48]{1,0:T(2,128)S(1)}, u32[]{:S(2)}, u32[]{:S(2)}) collective-permute-start(s32[2,48]{1,0:T(2,128)S(1)} %pad_add_fusion.1.refs_0_), channel_id=1, source_target_pairs={{0,2},{1,3},{2,0},{3,1},{4,6},{5,7},{6,4},{7,5},{8,10},{9,11},{10,... | collective-permute-start | bytes 1160 | tf_op jit(solution)/shard_map/ppermute | solution.py:44
  11.7 5.4 %collective-permute-start = (s32[2,48]{1,0:T(2,128)S(1)}, s32[2,48]{1,0:T(2,128)S(1)}, u32[]{:S(2)}, u32[]{:S(2)}) collective-permute-start(s32[2,48]{1,0:T(2,128)S(1)} %pad_add_fusion.1.refs_0_), channel_id=1, source_target_pairs={{0,1},{1,2},{2,3},{3,0},{4,5},{5,6},{6,7},{7,4},{8,9},{9,10},{10,1... | collective-permute-start | bytes 1160 | tf_op jit(solution)/shard_map/ppermute | solution.py:44
  12.7 29.5 %collective-permute-start.6 = (bf16[2,144,512]{2,1,0:T(8,128)(2,1)}, bf16[2,144,512]{2,1,0:T(8,128)(2,1)S(1)}, u32[]{:S(2)}, u32[]{:S(2)}) collective-permute-start(bf16[2,144,512]{2,1,0:T(8,128)(2,1)} %get-tuple-element.38), channel_id=1, source_target_pairs={{0,4},{4,0},{8,12},{12,8},{1,5},{5,1},{9,13},{13,9},{2,6},{6,2},{1... | collective-permute-start | bytes 884744 | tf_op jit(solution)/shard_map/ppermute | solution.py:37
  12.7 29.6 %collective-permute-start.7 = (bf16[2,144,512]{2,1,0:T(8,128)(2,1)}, bf16[2,144,512]{2,1,0:T(8,128)(2,1)S(1)}, u32[]{:S(2)}, u32[]{:S(2)}) collective-permute-start(bf16[2,144,512]{2,1,0:T(8,128)(2,1)} %get-tuple-element.39), channel_id=1, source_target_pairs={{0,8},{4,12},{8,0},{12,4},{1,9},{5,13},{9,1},{13,5},{2,10},{6,14},... | collective-permute-start | bytes 884744 | tf_op jit(solution)/shard_map/ppermute | solution.py:37
  15.5 1.6 copy-start.26
  15.5 26.8 %collective-permute-start.8 = (bf16[2,144,512]{2,1,0:T(8,128)(2,1)}, bf16[2,144,512]{2,1,0:T(8,128)(2,1)S(1)}, u32[]{:S(2)}, u32[]{:S(2)}) collective-permute-start(bf16[2,144,512]{2,1,0:T(8,128)(2,1)} %get-tuple-element.40), channel_id=1, source_target_pairs={{0,12},{4,8},{8,4},{12,0},{1,13},{5,9},{9,5},{13,1},{2,14},{6,10},... | collective-permute-start | bytes 884744 | tf_op jit(solution)/shard_map/ppermute | solution.py:37
  15.8 1.3 copy-start.27
  42.3 0.7 copy-start
  42.3 0.8 copy-start.1
  42.3 0.9 copy-start.2
  54.1 4.9 %collective-permute-start.11 = (f32[12,512]{1,0:T(8,128)}, f32[12,512]{1,0:T(8,128)S(1)}, u32[]{:S(2)}, u32[]{:S(2)}) collective-permute-start(f32[12,512]{1,0:T(8,128)} %get-tuple-element.44.refs_0_), channel_id=1, source_target_pairs={{0,3},{1,0},{2,1},{3,2},{4,7},{5,4},{6,5},{7,6},{8,11},{9,8},{10,9... | collective-permute-start | bytes 73736 | tf_op jit(solution)/shard_map/ppermute | solution.py:44
  57.1 5.0 %collective-permute-start.10 = (f32[12,512]{1,0:T(8,128)}, f32[12,512]{1,0:T(8,128)S(1)}, u32[]{:S(2)}, u32[]{:S(2)}) collective-permute-start(f32[12,512]{1,0:T(8,128)} %get-tuple-element.44.refs_0_), channel_id=1, source_target_pairs={{0,2},{1,3},{2,0},{3,1},{4,6},{5,7},{6,4},{7,5},{8,10},{9,11},{10,... | collective-permute-start | bytes 73736 | tf_op jit(solution)/shard_map/ppermute | solution.py:44
  57.4 5.9 %collective-permute-start.9 = (f32[12,512]{1,0:T(8,128)}, f32[12,512]{1,0:T(8,128)S(1)}, u32[]{:S(2)}, u32[]{:S(2)}) collective-permute-start(f32[12,512]{1,0:T(8,128)} %get-tuple-element.44.refs_0_), channel_id=1, source_target_pairs={{0,1},{1,2},{2,3},{3,0},{4,5},{5,6},{6,7},{7,4},{8,9},{9,10},{10,1... | collective-permute-start | bytes 73736 | tf_op jit(solution)/shard_map/ppermute | solution.py:44
  59.1 4.3 %copy-start.21 = (f32[12,512]{1,0:T(8,128)}, f32[12,512]{1,0:T(8,128)S(1)}, u32[]{:S(2)}) copy-start(f32[12,512]{1,0:T(8,128)S(1)} %collective-permute-done.11.refs_3_) | copy-start | bytes 73732
  62.2 1.1 copy-start.22
  65.5 5.9 %collective-permute-start.14 = (f32[24,512]{1,0:T(8,128)}, f32[24,512]{1,0:T(8,128)S(1)}, u32[]{:S(2)}, u32[]{:S(2)}) collective-permute-start(f32[24,512]{1,0:T(8,128)} %shard_map.68.refs_0_), channel_id=1, source_target_pairs={{0,12},{4,8},{8,4},{12,0},{1,13},{5,9},{9,5},{13,1},{2,14},{6,10},... | collective-permute-start | bytes 147464 | tf_op jit(solution)/shard_map/ppermute | solution.py:37
  69.3 4.3 %collective-permute-start.13 = (f32[24,512]{1,0:T(8,128)}, f32[24,512]{1,0:T(8,128)S(1)}, u32[]{:S(2)}, u32[]{:S(2)}) collective-permute-start(f32[24,512]{1,0:T(8,128)} %shard_map.68.refs_0_), channel_id=1, source_target_pairs={{0,8},{4,12},{8,0},{12,4},{1,9},{5,13},{9,1},{13,5},{2,10},{6,14},... | collective-permute-start | bytes 147464 | tf_op jit(solution)/shard_map/ppermute | solution.py:37
  69.3 4.3 %collective-permute-start.12 = (f32[24,512]{1,0:T(8,128)}, f32[24,512]{1,0:T(8,128)S(1)}, u32[]{:S(2)}, u32[]{:S(2)}) collective-permute-start(f32[24,512]{1,0:T(8,128)} %shard_map.68.refs_0_), channel_id=1, source_target_pairs={{0,4},{4,0},{8,12},{12,8},{1,5},{5,1},{9,13},{13,9},{2,6},{6,2},{1... | collective-permute-start | bytes 147464 | tf_op jit(solution)/shard_map/ppermute | solution.py:37
  71.3 2.2 %copy-start.18 = (f32[24,512]{1,0:T(8,128)}, f32[24,512]{1,0:T(8,128)S(1)}, u32[]{:S(2)}) copy-start(f32[24,512]{1,0:T(8,128)S(1)} %collective-permute-done.14.refs_3_) | copy-start | bytes 147460
  73.6 0.6 copy-start.19
  83.0 16.4 %collective-permute-start.15 = (bf16[2,64,512]{2,1,0:T(8,128)(2,1)}, bf16[2,64,512]{2,1,0:T(8,128)(2,1)S(1)}, u32[]{:S(2)}, u32[]{:S(2)}) collective-permute-start(bf16[2,64,512]{2,1,0:T(8,128)(2,1)} %get-tuple-element.48), channel_id=1, source_target_pairs={{0,4},{4,0},{8,12},{12,8},{1,5},{5,1},{9,13},{13,9},{2,6},{6,2},{1... | collective-permute-start | bytes 393224 | tf_op jit(solution)/shard_map/ppermute | solution.py:37
  83.1 16.4 %collective-permute-start.16 = (bf16[2,64,512]{2,1,0:T(8,128)(2,1)}, bf16[2,64,512]{2,1,0:T(8,128)(2,1)S(1)}, u32[]{:S(2)}, u32[]{:S(2)}) collective-permute-start(bf16[2,64,512]{2,1,0:T(8,128)(2,1)} %get-tuple-element.49), channel_id=1, source_target_pairs={{0,8},{4,12},{8,0},{12,4},{1,9},{5,13},{9,1},{13,5},{2,10},{6,14},... | collective-permute-start | bytes 393224 | tf_op jit(solution)/shard_map/ppermute | solution.py:37
  83.2 16.3 %collective-permute-start.17 = (bf16[2,64,512]{2,1,0:T(8,128)(2,1)}, bf16[2,64,512]{2,1,0:T(8,128)(2,1)S(1)}, u32[]{:S(2)}, u32[]{:S(2)}) collective-permute-start(bf16[2,64,512]{2,1,0:T(8,128)(2,1)} %get-tuple-element.50), channel_id=1, source_target_pairs={{0,12},{4,8},{8,4},{12,0},{1,13},{5,9},{9,5},{13,1},{2,14},{6,10},... | collective-permute-start | bytes 393224 | tf_op jit(solution)/shard_map/ppermute | solution.py:37
  99.5 0.6 copy-start.12
  99.5 0.7 copy-start.13
  99.5 0.7 copy-start.14
  107.0 6.4 %collective-permute-start.23 = (f32[64,64]{1,0:T(8,128)}, f32[64,64]{1,0:T(8,128)S(1)}, u32[]{:S(2)}, u32[]{:S(2)}) collective-permute-start(f32[64,64]{1,0:T(8,128)} %get-tuple-element.52), channel_id=1, source_target_pairs={{0,3},{1,0},{2,1},{3,2},{4,7},{5,4},{6,5},{7,6},{8,11},{9,8},{10,9... | collective-permute-start | bytes 49160 | tf_op jit(solution)/shard_map/ppermute | solution.py:44
  108.5 5.6 %collective-permute-start.22 = (f32[64,64]{1,0:T(8,128)}, f32[64,64]{1,0:T(8,128)S(1)}, u32[]{:S(2)}, u32[]{:S(2)}) collective-permute-start(f32[64,64]{1,0:T(8,128)} %get-tuple-element.52), channel_id=1, source_target_pairs={{0,2},{1,3},{2,0},{3,1},{4,6},{5,7},{6,4},{7,5},{8,10},{9,11},{10,... | collective-permute-start | bytes 49160 | tf_op jit(solution)/shard_map/ppermute | solution.py:44
  108.5 6.2 %collective-permute-start.21 = (f32[64,64]{1,0:T(8,128)}, f32[64,64]{1,0:T(8,128)S(1)}, u32[]{:S(2)}, u32[]{:S(2)}) collective-permute-start(f32[64,64]{1,0:T(8,128)} %get-tuple-element.52), channel_id=1, source_target_pairs={{0,1},{1,2},{2,3},{3,0},{4,5},{5,6},{6,7},{7,4},{8,9},{9,10},{10,1... | collective-permute-start | bytes 49160 | tf_op jit(solution)/shard_map/ppermute | solution.py:44
  109.1 24.8 %collective-permute-start.20 = (bf16[4,64,512]{2,1,0:T(8,128)(2,1)}, bf16[4,64,512]{2,1,0:T(8,128)(2,1)S(1)}, u32[]{:S(2)}, u32[]{:S(2)}) collective-permute-start(bf16[4,64,512]{2,1,0:T(8,128)(2,1)} %get-tuple-element.53.refs_5_.refs_6_), channel_id=1, source_target_pairs={{0,3},{1,0},{2,1},{3,2},{4,7},{5,4},{6,5},{7,6},{8,11},{9,8},{10,9... | collective-permute-start | bytes 786440 | tf_op jit(solution)/shard_map/ppermute | solution.py:44
  112.3 24.9 %collective-permute-start.19 = (bf16[4,64,512]{2,1,0:T(8,128)(2,1)}, bf16[4,64,512]{2,1,0:T(8,128)(2,1)S(1)}, u32[]{:S(2)}, u32[]{:S(2)}) collective-permute-start(bf16[4,64,512]{2,1,0:T(8,128)(2,1)} %get-tuple-element.53.refs_5_.refs_6_), channel_id=1, source_target_pairs={{0,2},{1,3},{2,0},{3,1},{4,6},{5,7},{6,4},{7,5},{8,10},{9,11},{10,... | collective-permute-start | bytes 786440 | tf_op jit(solution)/shard_map/ppermute | solution.py:44
  113.4 23.8 %collective-permute-start.18 = (bf16[4,64,512]{2,1,0:T(8,128)(2,1)}, bf16[4,64,512]{2,1,0:T(8,128)(2,1)S(1)}, u32[]{:S(2)}, u32[]{:S(2)}) collective-permute-start(bf16[4,64,512]{2,1,0:T(8,128)(2,1)} %get-tuple-element.53.refs_5_.refs_6_), channel_id=1, source_target_pairs={{0,1},{1,2},{2,3},{3,0},{4,5},{5,6},{6,7},{7,4},{8,9},{9,10},{10,1... | collective-permute-start | bytes 786440 | tf_op jit(solution)/shard_map/ppermute | solution.py:44
  115.5 1.3 collective-permute-start.24
  116.8 9.8 %collective-permute-start.25 = (f32[64,64]{1,0:T(8,128)S(1)}, f32[64,64]{1,0:T(8,128)S(1)}, u32[]{:S(2)}, u32[]{:S(2)}) collective-permute-start(f32[64,64]{1,0:T(8,128)S(1)} %add.30), channel_id=1, source_target_pairs={{0,8},{4,12},{8,0},{12,4},{1,9},{5,13},{9,1},{13,5},{2,10},{6,14},... | collective-permute-start | bytes 49160 | tf_op jit(solution)/shard_map/ppermute | solution.py:52
  134.0 3.3 %copy-start.3 = (bf16[4,64,512]{2,1,0:T(8,128)(2,1)}, bf16[4,64,512]{2,1,0:T(8,128)(2,1)S(1)}, u32[]{:S(2)}) copy-start(bf16[4,64,512]{2,1,0:T(8,128)(2,1)S(1)} %collective-permute-done.20.refs_8_.refs_9_) | copy-start | bytes 786436
  137.2 0.7 copy-start.4
  137.9 0.7 copy-start.5
  145.0 2.4 %collective-permute-start.26 = (bf16[2,64,512]{2,1,0:T(8,128)(2,1)}, bf16[2,64,512]{2,1,0:T(8,128)(2,1)S(1)}, u32[]{:S(2)}, u32[]{:S(2)}) collective-permute-start(bf16[2,64,512]{2,1,0:T(8,128)(2,1)} %get-tuple-element.59), channel_id=1, source_target_pairs={{0,4},{4,0},{8,12},{12,8},{1,5},{5,1},{9,13},{13,9},{2,6},{6,2},{1... | collective-permute-start | bytes 393224 | tf_op jit(solution)/shard_map/ppermute | solution.py:37
  145.0 16.5 %collective-permute-start.27 = (bf16[2,64,512]{2,1,0:T(8,128)(2,1)}, bf16[2,64,512]{2,1,0:T(8,128)(2,1)S(1)}, u32[]{:S(2)}, u32[]{:S(2)}) collective-permute-start(bf16[2,64,512]{2,1,0:T(8,128)(2,1)} %get-tuple-element.60), channel_id=1, source_target_pairs={{0,8},{4,12},{8,0},{12,4},{1,9},{5,13},{9,1},{13,5},{2,10},{6,14},... | collective-permute-start | bytes 393224 | tf_op jit(solution)/shard_map/ppermute | solution.py:37
  145.1 16.4 %collective-permute-start.28 = (bf16[2,64,512]{2,1,0:T(8,128)(2,1)}, bf16[2,64,512]{2,1,0:T(8,128)(2,1)S(1)}, u32[]{:S(2)}, u32[]{:S(2)}) collective-permute-start(bf16[2,64,512]{2,1,0:T(8,128)(2,1)} %get-tuple-element.61), channel_id=1, source_target_pairs={{0,12},{4,8},{8,4},{12,0},{1,13},{5,9},{9,5},{13,1},{2,14},{6,10},... | collective-permute-start | bytes 393224 | tf_op jit(solution)/shard_map/ppermute | solution.py:37
  146.9 14.7 %collective-permute-start.29 = (bf16[2,64,512]{2,1,0:T(8,128)(2,1)}, bf16[2,64,512]{2,1,0:T(8,128)(2,1)S(1)}, u32[]{:S(2)}, u32[]{:S(2)}) collective-permute-start(bf16[2,64,512]{2,1,0:T(8,128)(2,1)} %get-tuple-element.62), channel_id=1, source_target_pairs={{0,4},{4,0},{8,12},{12,8},{1,5},{5,1},{9,13},{13,9},{2,6},{6,2},{1... | collective-permute-start | bytes 393224 | tf_op jit(solution)/shard_map/ppermute | solution.py:37
  147.2 14.3 %collective-permute-start.30 = (bf16[2,64,512]{2,1,0:T(8,128)(2,1)}, bf16[2,64,512]{2,1,0:T(8,128)(2,1)S(1)}, u32[]{:S(2)}, u32[]{:S(2)}) collective-permute-start(bf16[2,64,512]{2,1,0:T(8,128)(2,1)} %get-tuple-element.63), channel_id=1, source_target_pairs={{0,8},{4,12},{8,0},{12,4},{1,9},{5,13},{9,1},{13,5},{2,10},{6,14},... | collective-permute-start | bytes 393224 | tf_op jit(solution)/shard_map/ppermute | solution.py:37
  147.4 14.3 %copy-start.6 = (bf16[2,64,512]{2,1,0:T(8,128)(2,1)}, bf16[2,64,512]{2,1,0:T(8,128)(2,1)S(1)}, u32[]{:S(2)}) copy-start(bf16[2,64,512]{2,1,0:T(8,128)(2,1)S(1)} %collective-permute-done.26.refs_8_) | copy-start | bytes 393220
  147.4 14.2 %collective-permute-start.31 = (bf16[2,64,512]{2,1,0:T(8,128)(2,1)}, bf16[2,64,512]{2,1,0:T(8,128)(2,1)S(1)}, u32[]{:S(2)}, u32[]{:S(2)}) collective-permute-start(bf16[2,64,512]{2,1,0:T(8,128)(2,1)} %get-tuple-element.64), channel_id=1, source_target_pairs={{0,12},{4,8},{8,4},{12,0},{1,13},{5,9},{9,5},{13,1},{2,14},{6,10},... | collective-permute-start | bytes 393224 | tf_op jit(solution)/shard_map/ppermute | solution.py:37
  161.5 0.7 copy-start.7
  161.5 0.7 copy-start.8
  161.6 0.7 copy-start.9
  161.6 0.7 copy-start.10
  162.3 0.7 copy-start.11
  170.8 1.5 collective-permute-start.32
  173.0 3.9 %collective-permute-start.33 = (f32[64,64]{1,0:T(8,128)S(1)}, f32[64,64]{1,0:T(8,128)S(1)}, u32[]{:S(2)}, u32[]{:S(2)}) collective-permute-start(f32[64,64]{1,0:T(8,128)S(1)} %add.32), channel_id=1, source_target_pairs={{0,8},{4,12},{8,0},{12,4},{1,9},{5,13},{9,1},{13,5},{2,10},{6,14},... | collective-permute-start | bytes 49160 | tf_op jit(solution)/shard_map/ppermute | solution.py:52
  176.9 9.3 %collective-permute-start.34 = (f32[64,64]{1,0:T(8,128)S(1)}, f32[64,64]{1,0:T(8,128)S(1)}, u32[]{:S(2)}, u32[]{:S(2)}) collective-permute-start(f32[64,64]{1,0:T(8,128)S(1)} %add.33), channel_id=1, source_target_pairs={{0,1},{1,0},{2,3},{3,2},{4,5},{5,4},{6,7},{7,6},{8,9},{9,8},{10,11... | collective-permute-start | bytes 49160 | tf_op jit(solution)/shard_map/ppermute | solution.py:52
  186.2 4.8 %collective-permute-start.35 = (f32[64,64]{1,0:T(8,128)S(1)}, f32[64,64]{1,0:T(8,128)S(1)}, u32[]{:S(2)}, u32[]{:S(2)}) collective-permute-start(f32[64,64]{1,0:T(8,128)S(1)} %add.34), channel_id=1, source_target_pairs={{0,2},{1,3},{2,0},{3,1},{4,6},{5,7},{6,4},{7,5},{8,10},{9,11},{10,... | collective-permute-start | bytes 49160 | tf_op jit(solution)/shard_map/ppermute | solution.py:52
  199.5 6.3 %collective-permute-start.36 = (bf16[4,16,512]{2,1,0:T(8,128)(2,1)}, bf16[4,16,512]{2,1,0:T(8,128)(2,1)S(1)}, u32[]{:S(2)}, u32[]{:S(2)}) collective-permute-start(bf16[4,16,512]{2,1,0:T(8,128)(2,1)} %get-tuple-element.68), channel_id=1, source_target_pairs={{0,1},{1,2},{2,3},{3,0},{4,5},{5,6},{6,7},{7,4},{8,9},{9,10},{10,1... | collective-permute-start | bytes 196616 | tf_op jit(solution)/shard_map/ppermute | solution.py:872
  201.5 5.7 %collective-permute-start.37 = (bf16[4,16,512]{2,1,0:T(8,128)(2,1)}, bf16[4,16,512]{2,1,0:T(8,128)(2,1)S(1)}, u32[]{:S(2)}, u32[]{:S(2)}) collective-permute-start(bf16[4,16,512]{2,1,0:T(8,128)(2,1)} %get-tuple-element.69), channel_id=1, source_target_pairs={{0,2},{1,3},{2,0},{3,1},{4,6},{5,7},{6,4},{7,5},{8,10},{9,11},{10,... | collective-permute-start | bytes 196616 | tf_op jit(solution)/shard_map/ppermute | solution.py:872
  201.7 5.4 %collective-permute-start.38 = (bf16[4,16,512]{2,1,0:T(8,128)(2,1)}, bf16[4,16,512]{2,1,0:T(8,128)(2,1)S(1)}, u32[]{:S(2)}, u32[]{:S(2)}) collective-permute-start(bf16[4,16,512]{2,1,0:T(8,128)(2,1)} %get-tuple-element.70), channel_id=1, source_target_pairs={{0,3},{1,0},{2,1},{3,2},{4,7},{5,4},{6,5},{7,6},{8,11},{9,8},{10,9... | collective-permute-start | bytes 196616 | tf_op jit(solution)/shard_map/ppermute | solution.py:872
  205.7 1.4 copy-start.15
  207.1 0.7 copy-start.17
  (4 other events, 2.4 us)
